TPU v7x, 512 devices: a whole 4x4x16 slice. The times are simulated.
512 devices in a mesh: ctx: 128 (over z, x, core), tp: 4 (over y).
Axes of the slice: x: 4, y: 4, z: 16, core: 2. Of those that a mesh axis runs over, the one named last changes fastest.
Arguments:
- resid: bfloat16 [16384, 8192], P('ctx', 'tp'), may hold values from -64 to 64
- q_mr: bfloat16 [16384, 8192], P('ctx', 'tp'), may hold values from -4 to 4
- k_mr: bfloat16 [16384, 8192], P('ctx', 'tp'), may hold values from -4 to 4
- v_mr: bfloat16 [16384, 8192], P('ctx', 'tp'), may hold values from -4 to 4
- mr_taps: bfloat16 [512, 128], P('tp'), may hold values from -0.5 to 0.5
- norm_gain: bfloat16 [8192], P('tp'), may hold values from 0.099609375 to 1.8984375
- q_lr: bfloat16 [16384, 8192], P('ctx', 'tp'), may hold values from -4 to 4
- k_lr: bfloat16 [16384, 8192], P('ctx', 'tp'), may hold values from -4 to 4
- pole_rate: float32 [16, 512], P(None, 'tp'), may hold values from 0 to 1, as said below
- residue: float32 [16, 512], P(None, 'tp'), may hold values from -3 to 3
Outputs:
- mixed: bfloat16 [16384, 8192], P('ctx', 'tp')
- lr_out: bfloat16 [16384, 8192], P('ctx', 'tp')
Inputs may be any that keep to these rules, and one draw needn't show every extreme that they name: `pole_rate`: every rate is positive.
All inputs are finite; a program needn't handle non-finite values.
Results may differ from a plain program's by a relative error of at most 0.0052.
Values may be sent and summed in bfloat16 or wider, within the bound.
A program may use at most 128 MiB of HBM per device.

v0:
```python
import jax
import jax.numpy as jnp
from jax import lax
from jax.sharding import PartitionSpec as P

D = 8192


HIGHEST_MODE = lax.Precision.HIGHEST


def passed_along(x, axis, by):
    peers = lax.axis_size(axis)
    pairs = [(i, i + by) for i in range(peers) if 0 <= i + by < peers]
    return lax.ppermute(x, axis, pairs)


def carried_in(part, axis, combine, identity):
    place = lax.axis_index(axis)
    gathered = jax.tree.map(lambda a: lax.all_gather(a, axis), part)
    state = jax.tree.map(lambda a, e: jnp.zeros_like(a) + jnp.asarray(e, a.dtype), part, identity)

    def one(step, state):
        return combine(
            state, jax.tree.map(lambda a: lax.dynamic_index_in_dim(a, step, 0, False), gathered)
        )

    return lax.fori_loop(0, place, one, state)


def banded(vector, out_rows):
    length = vector.shape[-1]
    span_cols = out_rows + length - 1
    padding = jnp.zeros(vector.shape[:-1] + (span_cols + 1 - length,), vector.dtype)
    line = jnp.concatenate([vector, padding], axis=-1)
    tiled = jnp.tile(line, (1,) * (vector.ndim - 1) + (out_rows,))
    return tiled[..., : out_rows * span_cols].reshape(vector.shape[:-1] + (out_rows, span_cols))


def modal_tables(pole_rate, residue, tok_rows):
    weights_eff = residue * jnp.sqrt(-jnp.expm1(-2.0 * pole_rate))
    positions = jnp.arange(tok_rows, dtype=jnp.float32)
    powers = jnp.exp(-pole_rate[:, :, None] * positions)
    impulse = jnp.sum(weights_eff[:, :, None] * powers, axis=0)
    square = banded(impulse[:, ::-1], tok_rows)[:, :, tok_rows - 1 :]
    entry = weights_eff[:, :, None] * powers * jnp.exp(-pole_rate)[:, :, None]
    leaving = powers[:, :, ::-1]
    through = jnp.exp(-pole_rate * tok_rows)
    return (square, entry, leaving, through)


def tokens_last(rows, local_groups, group_size):
    row_count = rows.shape[0]
    return jnp.transpose(rows.reshape(row_count, local_groups, group_size), (1, 2, 0))


def tokens_first(grouped, channels):
    return jnp.transpose(grouped, (2, 0, 1)).reshape(grouped.shape[2], channels)


def per_device(resid, q_mr, k_mr, v_mr, mr_taps, norm_gain, q_lr, k_lr, pole_rate, residue):
    tok_rows, channels = resid.shape
    local_groups, tap_count = mr_taps.shape
    group_size = channels // local_groups
    mr_in = (k_mr.astype(jnp.float32) * v_mr.astype(jnp.float32)).astype(jnp.bfloat16)
    rim_rows = passed_along(mr_in[tok_rows - tap_count + 1 :], "ctx", 1)
    window = jnp.concatenate([rim_rows, mr_in], axis=0)
    window = tokens_last(window, local_groups, group_size)
    kernel = banded(mr_taps[:, ::-1], tok_rows)
    mr_conv = jnp.einsum("gtr,gcr->gct", kernel, window, preferred_element_type=jnp.float32)
    mr_conv = tokens_first(mr_conv, channels)
    mixed = (resid.astype(jnp.float32) + q_mr.astype(jnp.float32) * mr_conv).astype(jnp.bfloat16)
    mixed_f = mixed.astype(jnp.float32)
    square_sum = lax.psum(jnp.sum(mixed_f * mixed_f, axis=1), "tp")
    normed = mixed_f * lax.rsqrt(square_sum[:, None] / D + 1e-06) * norm_gain.astype(jnp.float32)
    lr_in = tokens_last(k_lr.astype(jnp.float32) * normed, local_groups, group_size)
    square, entry, leaving, through = modal_tables(pole_rate, residue, tok_rows)
    local = jnp.einsum("gts,gcs->gct", square, lr_in, precision=HIGHEST_MODE)
    state_end = jnp.einsum("pgs,gcs->pgc", leaving, lr_in, precision=HIGHEST_MODE)
    state_end = state_end.reshape(state_end.shape[0], channels)

    def combine(former, latter):
        factor = jnp.repeat(latter[0], group_size, axis=1)
        return (former[0] * latter[0], factor * former[1] + latter[1])

    identity = (jnp.ones_like(through), jnp.zeros_like(state_end))
    scanned = carried_in((through, state_end), "ctx", combine, identity)
    carried = scanned[1]
    carried = carried.reshape(carried.shape[0], local_groups, group_size)
    incoming = jnp.einsum("pgt,pgc->gct", entry, carried, precision=HIGHEST_MODE)
    lr_conv = tokens_first(local + incoming, channels)
    lr_out = (q_lr.astype(jnp.float32) * lr_conv).astype(jnp.bfloat16)
    return (mixed, lr_out)


def solution(mesh):
    placed = (
        P("ctx", "tp"),
        P("ctx", "tp"),
        P("ctx", "tp"),
        P("ctx", "tp"),
        P("tp", None),
        P("tp"),
        P("ctx", "tp"),
        P("ctx", "tp"),
        P(None, "tp"),
        P(None, "tp"),
    )
    return jax.shard_map(
        per_device,
        mesh=mesh,
        in_specs=placed,
        out_specs=(P("ctx", "tp"), P("ctx", "tp")),
        check_vma=False,
    )
```

profile of v0, /device:TPU:487, one launch (start us, length us, event | category | flops | bytes accessed | tf_op | source)
XLA Modules:
  0.0 649.0 jit_solution(9956263974648795304)
XLA Ops:
  7.2 1.3 multiply_convert_fusion.1
  9.5 1.3 collective-permute-start
  10.8 1.3 negate_exponential_fusion
  14.4 3.8 tile.8
  18.2 12.3 %copy.44 = bf16[16,8,128,256]{3,1,2,0:T(8,128)(2,1)} copy(bf16[16,8,128,256]{3,2,1,0:T(8,128)(2,1)} %bitcast.43) | data formatting | bytes 16777216
  30.5 7.1 %slice.17 = bf16[128,32640]{1,0:T(8,128)(2,1)} slice(bf16[128,32768]{1,0:T(8,128)(2,1)} %bitcast.44), slice={[0:128], [0:32640]} | slice | bytes 16711680 | tf_op jit(solution)/shard_map/slice | solution.py:37
  37.7 29.6 %reshape.47 = bf16[128,128,255]{2,1,0:T(8,128)(2,1)} reshape(bf16[128,32640]{1,0:T(8,128)(2,1)} %slice.17) | data formatting | bytes 16711680 | tf_op jit(solution)/shard_map/reshape | solution.py:37
  67.3 1.0 copy.32
  68.3 1.0 copy.33
  69.6 2.3 pad_maximum_fusion
  71.9 1.5 copy.34
  73.4 5.7 fusion.13
  79.4 8.9 %psum.7 = f32[128]{0:T(128)S(1)} all-reduce(f32[128]{0:T(128)S(1)} %get-tuple-element.61), channel_id=1, replica_groups=mesh['ctx'=128,'tp'=4] {'tp'}, use_global_device_ids=true, to_apply=%region_1.0 | all-reduce | flops 128 | bytes 1024 | tf_op jit(solution)/shard_map/psum | solution.py:74
  88.7 2.7 fusion.14
  91.4 2.2 copy.38
  93.7 1.3 tile.20
  95.0 20.7 %copy.45 = f32[16,8,128,256]{3,1,2,0:T(8,128)S(1)} copy(f32[16,8,128,256]{3,2,1,0:T(8,128)S(1)} %bitcast.41) | data formatting | bytes 33554432
  115.7 6.0 slice.18
  121.7 28.9 %reshape.50 = f32[128,128,255]{2,1,0:T(8,128)} reshape(f32[128,32640]{1,0:T(8,128)} %slice.18) | data formatting | bytes 33423360 | tf_op jit(solution)/shard_map/reshape | solution.py:37
  151.3 1.0 copy.42
  152.3 16.2 %fusion = f32[128,16,128]{2,1,0:T(8,128)S(1)} fusion(f32[128,16,128]{2,1,0:T(8,128)S(1)} %bitcast.46, f32[128,128,255]{2,1,0:T(8,128)} %reshape.50), kind=kOutput, calls=%fused_computation.2 | convolution fusion | flops 402653184 | bytes 10485760 | tf_op jit(solution)/shard_map/gts,gcs->gct/dot_general | solution.py:78
  168.5 129.8 %all-gather.4.cloned.1.call-done = f32[128,16,2048]{2,1,0:T(8,128)} async-done(((f32[1,16,2048]{2,1,0:T(8,128)}), f32[128,16,2048]{2,1,0:T(8,128)}) %all-gather.4.cloned.1.call-update) | async-done | bytes 16777232 | tf_op jit(solution)/shard_map/all_gather | solution.py:20
  298.3 338.0 %while.12 = (s32[]{:T(128)}, f32[16,2048]{1,0:T(8,128)S(1)}, s32[]{:T(128)}, f32[128,16,128]{2,1,0:T(8,128)}, f32[128,16,2048]{2,1,0:T(8,128)}, /*index=5*/s32[]{:T(128)}, s32[]{:T(128)}, s32[]{:T(128)}) while((s32[]{:T(128)}, f32[16,2048]{1,0:T(8,128)S(1)}, s32[]{:T(128)}, f32[128,16,128]{2,1,0:T(8,128)}, f32[128,16,2048]{2,1,0:T(8,128)}, ...), condition=%wide.region_4.5_spmd, body=%wide.region_3.4_spmd.sunk | while | flops 65541 | bytes 942207 | solution.py:28
  302.7 1.0 bitcast_add_fusion.2
  308.0 1.0 bitcast_add_fusion.2
  310.7 1.0 bitcast_add_fusion.2
  316.0 1.0 bitcast_add_fusion.2
  318.7 1.0 bitcast_add_fusion.2
  324.0 1.0 bitcast_add_fusion.2
  329.3 1.0 bitcast_add_fusion.2
  332.0 1.0 bitcast_add_fusion.2
  337.3 1.0 bitcast_add_fusion.2
  340.0 1.0 bitcast_add_fusion.2
  345.3 1.0 bitcast_add_fusion.2
  347.9 1.0 bitcast_add_fusion.2
  353.3 1.0 bitcast_add_fusion.2
  358.6 1.0 bitcast_add_fusion.2
  361.2 1.0 bitcast_add_fusion.2
  366.6 1.0 bitcast_add_fusion.2
  369.2 1.0 bitcast_add_fusion.2
  374.5 1.0 bitcast_add_fusion.2
  379.9 1.0 bitcast_add_fusion.2
  382.5 1.0 bitcast_add_fusion.2
  387.9 1.0 bitcast_add_fusion.2
  390.5 1.0 bitcast_add_fusion.2
  395.8 1.0 bitcast_add_fusion.2
  398.5 1.0 bitcast_add_fusion.2
  403.8 1.0 bitcast_add_fusion.2
  409.1 1.0 bitcast_add_fusion.2
  411.8 1.0 bitcast_add_fusion.2
  417.1 1.0 bitcast_add_fusion.2
  419.8 1.0 bitcast_add_fusion.2
  425.1 1.0 bitcast_add_fusion.2
  430.4 1.0 bitcast_add_fusion.2
  433.1 1.0 bitcast_add_fusion.2
  438.4 1.0 bitcast_add_fusion.2
  441.1 1.0 bitcast_add_fusion.2
  446.4 1.0 bitcast_add_fusion.2
  449.1 1.0 bitcast_add_fusion.2
  454.4 1.0 bitcast_add_fusion.2
  459.7 1.0 bitcast_add_fusion.2
  462.4 1.0 bitcast_add_fusion.2
  636.6 3.2 convolution_add_fusion
  640.2 1.9 multiply_convert_fusion
  (505 shorter events, 301.4 us)
Async XLA Ops:
  7.2 161.4 %all-gather.6.cloned.1.call-start = ((), (), s32[]{:S(2)}) async-start(), calls=%async_computation.1 | async-start | bytes 1056768 | tf_op jit(solution)/shard_map/all_gather | solution.py:20
  9.5 60.1 %collective-permute-start = (bf16[127,2048]{1,0:T(8,128)(2,1)}, bf16[127,2048]{1,0:T(8,128)(2,1)}, u32[]{:S(2)}, u32[]{:S(2)}) collective-permute-start(bf16[127,2048]{1,0:T(8,128)(2,1)} %slice.16), channel_id=1, source_target_pairs={{0,4},{4,8},{8,12},{12,16},{16,20},{20,24},{24,28},{28,32},{32,36}... | collective-permute-start | bytes 1560584 | tf_op jit(solution)/shard_map/ppermute | solution.py:15
  12.1 286.2 %all-gather.4.cloned.1.call-start = ((), (), s32[]{:S(2)}) async-start(), calls=%async_computation | async-start | bytes 16908288 | tf_op jit(solution)/shard_map/all_gather | solution.py:20
  37.7 29.6 %copy-start.2 = (bf16[128,2048]{1,0:T(8,128)(2,1)S(1)}, bf16[128,2048]{1,0:T(8,128)(2,1)}, u32[]{:S(2)}) copy-start(bf16[128,2048]{1,0:T(8,128)(2,1)} %param.12) | copy-start | bytes 1572868
  37.7 30.6 %copy-start.3 = (bf16[128,2048]{1,0:T(8,128)(2,1)S(1)}, bf16[128,2048]{1,0:T(8,128)(2,1)}, u32[]{:S(2)}) copy-start(bf16[128,2048]{1,0:T(8,128)(2,1)} %param.13) | copy-start | bytes 1572868
  37.7 31.6 %copy-start.4 = (bf16[128,2048]{1,0:T(8,128)(2,1)S(1)}, bf16[128,2048]{1,0:T(8,128)(2,1)}, u32[]{:S(2)}) copy-start(bf16[128,2048]{1,0:T(8,128)(2,1)} %param.19) | copy-start | bytes 1572868
  37.7 31.9 %copy-start.5 = (bf16[2048]{0:T(1024)(128)(2,1)S(1)}, bf16[2048]{0:T(1024)(128)(2,1)}, u32[]{:S(2)}) copy-start(bf16[2048]{0:T(1024)(128)(2,1)} %param.17) | copy-start | bytes 12292
  73.3 5.7 copy-start
  73.4 5.7 copy-start.1
Sparse Core Ops, SparseCore 0:
  12.2 129.4 all-gather.5
  145.5 152.8 all-gather.3
where the time goes:
time: 657 us; the launch traced here: 649 us
  local copies, waits for them, and re-layouts  331 us (50%)
  other arithmetic  131 us (20%)
  waiting for transfers between devices  130 us (20%)
  matrix products  27.9 us (4%)
  between operations  14.2 us (2%)
  blocking collectives  8.91 us (1%)
    all_gather x2, waiting for transfers between devices, carried_in(): gathered = jax.tree.map(lambda a: lax.all_gather(a, axis), part)  130 us
    add x127, other arithmetic, combine(): return (former[0] * latter[0], factor * former[1] + latter[1])  123 us
    squeeze x127, local copies, waits for them, and re-layouts, one(): lax.dynamic_index_in_dim(a, step, 0, False)  89.2 us
    reshape x127, local copies, waits for them, and re-layouts, combine(): factor = jnp.repeat(latter[0], group_size, axis=1)  79.7 us
    reshape x2, local copies, waits for them, and re-layouts, banded(): tiled[..., :out_rows * span_cols]  58.5 us
    broadcast_in_dim x127, local copies, waits for them, and re-layouts, combine(): factor = jnp.repeat(latter[0], group_size, axis=1)  41.3 us
    unnamed x18, local copies, waits for them, and re-layouts  36.3 us
    dot_general x1, matrix products, per_device(): local = jnp.einsum('gts,gcs->gct', square, lr_in, precision=HIGHEST_MODE)  16.2 us
  transfers between devices with their start and end apart: 3, of which 1 were waited for; matrix products, arithmetic and copies ran while one was open for 23% of the time, Pallas kernels for 0%

commit v1 on v0

v1 whole, which is shorter than its diff:
```python
import functools

import jax
import jax.numpy as jnp
from jax import lax
from jax.experimental import pallas as pl
from jax.experimental.pallas import tpu as pltpu
from jax.sharding import PartitionSpec as P

F32 = jnp.float32
BF16 = jnp.bfloat16
MESH = pl.DeviceIdType.MESH

TOK = 128
LANES = 128
GROUP = 16
PER_TILE = LANES // GROUP
POLES = 16
BLOCK = 16
OWNERS = 8
CHUNKS = 4

OWNER_STEPS = ((1, 2), (0, 2), (1, 1), (1, 3), (0, 1), (0, 3), (1, 0), (0, 0))
BLOCK_STEPS = (4, 3, 5, 2, 6, 1, 7)


def shared_steps(rate, residue):
    y = 2.0 * rate
    series = jnp.ones_like(y)
    for order in range(10, 1, -1):
        series = 1.0 - series * y / order
    gap = jnp.where(y < 0.5, y * series, 1.0 - jnp.exp(-y))
    return residue * jnp.sqrt(gap)


def kernel(
    blocks,
    tp_size,
    resid_h, q_mr_h, k_mr_h, v_mr_h, taps_h, gain_h, q_lr_h, k_lr_h, rate_h, residue_h,
    mixed_h, out_h,
    k_mr, v_mr, resid, q_mr, k_lr, q_lr, taps, gain, rate, residue,
    window, mr_tab, lr_tab, leave_tab, entry_tab, taps_rev, weight_eff, impulse,
    mixed, gated, local, lr_out, squares, states, gathered, total, totals, carry_out, carry_in,
    kv_sem, in_sem, out_sem, halo_send, halo_recv, tp_send, tp_recv,
    own_send, own_recv, tot_send, tot_recv, back_send, back_recv,
):
    me = lax.axis_index("ctx")
    tp = lax.axis_index("tp")
    shards = blocks * BLOCK
    channels = k_mr.shape[1]
    tiles = channels // LANES
    wide = channels // CHUNKS
    block = me // BLOCK
    member = me % BLOCK
    base = block * BLOCK
    core = me % 2
    x_at = (me // 2) % 4
    z_at = (me // 8) % 2
    first = me == 0
    last = me == shards - 1
    is_owner = core == 1

    kv_copies = []
    for c in range(CHUNKS):
        cols = pl.ds(c * wide, wide)
        pair = []
        for i, (src, dst) in enumerate(((k_mr_h, k_mr), (v_mr_h, v_mr))):
            copy = pltpu.make_async_copy(src.at[:, cols], dst.at[:, cols], kv_sem.at[i, c])
            copy.start()
            pair.append(copy)
        kv_copies.append(pair)
    in_copies = {}
    for i, (name, src, dst) in enumerate((
        ("taps", taps_h, taps), ("rate", rate_h, rate), ("residue", residue_h, residue),
        ("resid", resid_h, resid), ("q_mr", q_mr_h, q_mr), ("k_lr", k_lr_h, k_lr),
        ("gain", gain_h, gain), ("q_lr", q_lr_h, q_lr),
    )):
        in_copies[name] = pltpu.make_async_copy(src, dst, in_sem.at[i])
        in_copies[name].start()

    totals[...] = jnp.zeros_like(totals)

    barrier = pltpu.get_barrier_semaphore()

    def greet(ctx, tp_to):
        pl.semaphore_signal(barrier, inc=1, device_id=(ctx, tp_to), device_id_type=MESH)

    @pl.when(jnp.logical_not(last))
    def _():
        greet(me + 1, tp)

    @pl.when(jnp.logical_not(first))
    def _():
        greet(me - 1, tp)

    for d in range(1, tp_size):
        greet(me, (tp + d) % tp_size)
    for dz, dx in OWNER_STEPS:
        chip = base + ((z_at + dz) % 2) * 8 + ((x_at + dx) % 4) * 2
        if (dz, dx) != (0, 0):
            greet(chip + 1, tp)

    @pl.when(is_owner)
    def _():
        for dz, dx in OWNER_STEPS:
            chip = base + ((z_at + dz) % 2) * 8 + ((x_at + dx) % 4) * 2
            greet(chip, tp)
        for d in range(1, blocks):
            greet(((block + d) % blocks) * BLOCK + member, tp)

    @pl.when(jnp.logical_not(is_owner))
    def _():
        greet(me + 1, tp)

    halo = []
    for c in range(CHUNKS):
        for copy in kv_copies[c]:
            copy.wait()
        cols = pl.ds(c * wide, wide)
        window[TOK:, cols] = (k_mr[:, cols].astype(F32) * v_mr[:, cols].astype(F32)).astype(BF16)
        if c == 0:
            ends = jnp.where(first, 0, 1) + jnp.where(last, 0, 1)
            near = jnp.where(is_owner, BLOCK - 1 + blocks - 1, OWNERS)
            pl.semaphore_wait(barrier, ends + near + (tp_size - 1))

        copy = pltpu.make_async_remote_copy(
            src_ref=window.at[pl.ds(TOK, TOK), cols],
            dst_ref=window.at[pl.ds(0, TOK), cols],
            send_sem=halo_send.at[c],
            recv_sem=halo_recv.at[c],
            device_id=(jnp.where(last, me - 1, me + 1), tp),
            device_id_type=MESH,
        )
        halo.append(copy)

        @pl.when(jnp.logical_not(last))
        def _():
            copy.start()

    @pl.when(first)
    def _():
        window[:TOK, :] = jnp.zeros((TOK, channels), BF16)

    row_of = lax.broadcasted_iota(jnp.int32, (TOK, TOK), 0)
    col_of = lax.broadcasted_iota(jnp.int32, (TOK, TOK), 1)
    diagonal = row_of == col_of
    causal = col_of <= row_of
    for name in ("taps", "rate", "residue"):
        in_copies[name].wait()
    flip = ((row_of + col_of) % TOK == 0).astype(BF16)
    taps_rev[...] = jnp.dot(taps[...], flip, preferred_element_type=F32)
    weight_eff[...] = shared_steps(rate[...], residue[...])

    def mr_tables(j, carry):
        for i in range(PER_TILE):
            g = j * PER_TILE + i
            line = jnp.broadcast_to(taps_rev[pl.ds(g, 1), :], (TOK, TOK))
            square = pltpu.roll(line, 0, 1, stride=1, stride_axis=0)
            rows = pl.ds(pl.multiple_of(g * TOK, TOK), TOK)
            mr_tab[rows, :TOK] = jnp.where(causal, 0.0, square).astype(BF16)
            mr_tab[rows, TOK:] = jnp.where(causal, square, 0.0).astype(BF16)
        return carry

    lax.fori_loop(0, tiles, mr_tables, 0, unroll=4)

    row_group = row_of // POLES
    rates = jnp.concatenate([rate[...]] * PER_TILE, axis=0)
    weights = jnp.concatenate([weight_eff[...]] * PER_TILE, axis=0)
    backward = (TOK - 1 - col_of).astype(F32)
    forward = (col_of + 1).astype(F32)

    def of_rows(j, values):
        here = col_of == row_group + j * PER_TILE
        return jnp.sum(jnp.where(here, values, 0.0), axis=1, keepdims=True)

    def leave_table(j, carry):
        leave = jnp.exp(-of_rows(j, rates) * backward)
        rows = pl.ds(pl.multiple_of(j * TOK, TOK), TOK)
        high = leave.astype(BF16)
        leave_tab[rows, :TOK] = high
        leave_tab[rows, TOK:] = (leave - high.astype(F32)).astype(BF16)
        weighted = of_rows(j, weights) * leave
        lines = [
            jnp.sum(weighted[i * POLES : (i + 1) * POLES], axis=0, keepdims=True)
            for i in range(PER_TILE)
        ]
        rows = pl.ds(pl.multiple_of(j * PER_TILE, PER_TILE), PER_TILE)
        impulse[rows, :] = pltpu.roll(jnp.concatenate(lines, axis=0), 1, 1)
        return carry

    lax.fori_loop(0, tiles, leave_table, 0, unroll=4)

    def lr_tables(j, carry):
        for i in range(PER_TILE):
            g = j * PER_TILE + i
            line = jnp.broadcast_to(impulse[pl.ds(g, 1), :], (TOK, TOK))
            square = pltpu.roll(line, 0, 1, stride=1, stride_axis=0)
            rows = pl.ds(pl.multiple_of(g * TOK, TOK), TOK)
            lr_tab[rows, :] = jnp.where(causal, square, 0.0).astype(BF16)
        return carry

    def entry_table(j, carry):
        entry = (of_rows(j, weights) * jnp.exp(-of_rows(j, rates) * forward)).T
        high = entry.astype(BF16)
        rows = pl.ds(pl.multiple_of(j * TOK, TOK), TOK)
        entry_tab[rows, :LANES] = high
        entry_tab[rows, LANES:] = (entry - high.astype(F32)).astype(BF16)
        return carry

    def own_lanes(stacked, rows):
        mask = lax.broadcasted_iota(jnp.int32, (rows, LANES), 1) // GROUP
        out = stacked[:rows]
        for i in range(1, PER_TILE):
            out = jnp.where(mask == i, stacked[i * rows : (i + 1) * rows], out)
        return out

    squares_sum = jnp.zeros((TOK, LANES), F32)
    for name in ("resid", "q_mr"):
        in_copies[name].wait()
    for c in range(CHUNKS):
        @pl.when(jnp.logical_not(first))
        def _():
            halo[c].wait_recv()

        def mr_tile(j, acc):
            cols = pl.ds(pl.multiple_of(j * LANES, LANES), LANES)
            rows = pl.ds(pl.multiple_of(j * PER_TILE * TOK, TOK), PER_TILE * TOK)
            stacked = jnp.dot(mr_tab[rows, :], window[:, cols], preferred_element_type=F32)
            conv = own_lanes(stacked, TOK)
            result = (resid[:, cols].astype(F32) + q_mr[:, cols].astype(F32) * conv).astype(BF16)
            mixed[:, cols] = result
            result = result.astype(F32)
            return acc + result * result

        per_chunk = tiles // CHUNKS
        squares_sum = lax.fori_loop(c * per_chunk, (c + 1) * per_chunk, mr_tile, squares_sum, unroll=True)

    row_sum = jnp.sum(squares_sum, axis=1, keepdims=True)
    line = jnp.sum(jnp.where(diagonal, row_sum, 0.0), axis=0, keepdims=True)
    squares[tp] = jnp.broadcast_to(line, (8, TOK))
    tp_copies = []
    for d in (2, 1, 3):
        copy = pltpu.make_async_remote_copy(
            src_ref=squares.at[tp],
            dst_ref=squares.at[tp],
            send_sem=tp_send.at[d],
            recv_sem=tp_recv.at[d],
            device_id=(me, (tp + d) % tp_size),
            device_id_type=MESH,
        )
        copy.start()
        tp_copies.append(copy)
    mixed_copy = pltpu.make_async_copy(mixed, mixed_h, out_sem.at[0])
    mixed_copy.start()
    for name in ("k_lr", "gain", "q_lr"):
        in_copies[name].wait()

    def gate_tile(j, carry):
        cols = pl.ds(pl.multiple_of(j * LANES, LANES), LANES)
        scaled = mixed[:, cols].astype(F32) * gain[:, cols].astype(F32)
        gated[:, cols] = scaled * k_lr[:, cols].astype(F32)
        return carry

    lax.fori_loop(0, tiles, gate_tile, 0, unroll=4)
    lax.fori_loop(0, tiles, lr_tables, 0, unroll=4)
    lax.fori_loop(0, tiles, entry_table, 0, unroll=4)
    for copy in tp_copies:
        copy.wait_recv()
    line = squares[0, :1, :]
    for d in range(1, tp_size):
        line = line + squares[d, :1, :]
    line = lax.rsqrt(line / (channels * tp_size) + 1e-06)
    scale = jnp.sum(jnp.where(diagonal, line, 0.0), axis=1, keepdims=True)

    lr_in = window

    own_copies = []
    for s, (dz, dx) in enumerate(OWNER_STEPS):
        z_to, x_to = (z_at + dz) % 2, (x_at + dx) % 4
        owner = z_to * 4 + x_to
        for half in range(2):
            j = owner * 2 + half
            cols = pl.ds(pl.multiple_of(j * LANES, LANES), LANES)
            value = (gated[:, cols] * scale).astype(BF16)
            lr_in[:TOK, cols] = value
            rows = pl.ds(pl.multiple_of(j * LANES, LANES), LANES)
            stacked = jnp.dot(
                leave_tab[rows, :], jnp.concatenate([value, value], axis=0), preferred_element_type=F32
            )
            states[s, half * POLES : (half + 1) * POLES, :] = own_lanes(stacked, POLES).astype(BF16)
        copy = pltpu.make_async_remote_copy(
            src_ref=states.at[s],
            dst_ref=gathered.at[member],
            send_sem=own_send.at[s],
            recv_sem=own_recv,
            device_id=(
                jnp.where(is_owner & ((dz, dx) == (0, 0)), me - 1, base + z_to * 8 + x_to * 2 + 1),
                tp,
            ),
            device_id_type=MESH,
        )
        own_copies.append(copy)
        if (dz, dx) == (0, 0):
            @pl.when(is_owner)
            def _():
                gathered[member] = states[s]

            @pl.when(jnp.logical_not(is_owner))
            def _():
                copy.start()
        else:
            copy.start()

    def lr_conv_tile(j, carry):
        cols = pl.ds(pl.multiple_of(j * LANES, LANES), LANES)
        rows = pl.ds(pl.multiple_of(j * PER_TILE * TOK, TOK), PER_TILE * TOK)
        stacked = jnp.dot(lr_tab[rows, :], lr_in[:TOK, cols], preferred_element_type=F32)
        local[:, cols] = own_lanes(stacked, TOK)
        return carry

    lax.fori_loop(0, tiles // 2, lr_conv_tile, 0, unroll=4)

    my_owner = z_at * 4 + x_at

    def total_copy(d, to):
        return pltpu.make_async_remote_copy(
            src_ref=total,
            dst_ref=totals.at[block],
            send_sem=tot_send.at[d],
            recv_sem=tot_recv.at[block],
            device_id=(to * BLOCK + member, tp),
            device_id_type=MESH,
        )

    back_steps = [(dz, dx, c) for dz, dx in OWNER_STEPS for c in (0, 1)]
    back_steps.remove((0, 0, 1))

    @pl.when(is_owner)
    def _():
        lane = lax.broadcasted_iota(jnp.int32, (LANES, 2 * LANES), 1)
        row = lax.broadcasted_iota(jnp.int32, (LANES, 2 * LANES), 0)
        spread = (row == my_owner * 2 * PER_TILE + lane // GROUP).astype(F32)
        wide_rate = jnp.dot(
            rate[...], spread, precision=lax.Precision.HIGHEST, preferred_element_type=F32
        )
        wide_rate = jnp.concatenate([wide_rate[:, :LANES], wide_rate[:, LANES:]], axis=0)
        through = jnp.exp(-wide_rate * TOK)
        through_block = jnp.exp(-wide_rate * (TOK * BLOCK))
        pltpu.make_async_copy(
            gathered.at[pl.ds(0, BLOCK - 1)], gathered.at[pl.ds(0, BLOCK - 1)], own_recv
        ).wait()
        state = jnp.zeros((2 * POLES, LANES), F32)
        for i in range(BLOCK):
            state = state * through + gathered[i].astype(F32)
        total[...] = state.astype(BF16)
        for d in BLOCK_STEPS:
            @pl.when(block + d < blocks)
            def _():
                total_copy(d, block + d).start()

        lax.fori_loop(tiles // 2, tiles, lr_conv_tile, 0, unroll=4)

        carried = jnp.zeros((2 * POLES, LANES), F32)
        for b in range(blocks - 1):
            @pl.when(b < block)
            def _():
                pltpu.make_async_copy(totals.at[b], totals.at[b], tot_recv.at[b]).wait()

        for b in range(blocks - 1):
            carried = jnp.where(b < block, carried * through_block + totals[b].astype(F32), carried)
        for i in range(BLOCK):
            carry_out[i] = carried.astype(BF16)
            if i < BLOCK - 1:
                carried = carried * through + gathered[i].astype(F32)
        for s, (dz, dx, c) in enumerate(back_steps):
            to = ((z_at + dz) % 2) * 8 + ((x_at + dx) % 4) * 2 + c
            pltpu.make_async_remote_copy(
                src_ref=carry_out.at[to],
                dst_ref=carry_in.at[my_owner],
                send_sem=back_send.at[s],
                recv_sem=back_recv,
                device_id=(base + to, tp),
                device_id_type=MESH,
            ).start()
        carry_in[my_owner] = carry_out[member]
        pltpu.make_async_copy(
            carry_in.at[pl.ds(0, OWNERS - 1)], carry_in.at[pl.ds(0, OWNERS - 1)], back_recv
        ).wait()

    @pl.when(jnp.logical_not(is_owner))
    def _():
        lax.fori_loop(tiles // 2, tiles, lr_conv_tile, 0, unroll=4)
        pltpu.make_async_copy(carry_in, carry_in, back_recv).wait()

    lane_group = lax.broadcasted_iota(jnp.int32, (POLES, LANES), 1) // GROUP
    pole_masks = [(lane_group == i).astype(F32).astype(BF16) for i in range(PER_TILE)]

    def out_tile(j, carry):
        cols = pl.ds(pl.multiple_of(j * LANES, LANES), LANES)
        rows = pl.ds(pl.multiple_of(j * TOK, TOK), TOK)
        came = carry_in[j // 2, pl.ds(pl.multiple_of((j % 2) * POLES, POLES), POLES), :]
        spread = [came * mask for mask in pole_masks]
        spread = jnp.concatenate(spread + spread, axis=0)
        incoming = jnp.dot(entry_tab[rows, :], spread, preferred_element_type=F32)
        conv = local[:, cols] + incoming
        lr_out[:, cols] = (q_lr[:, cols].astype(F32) * conv).astype(BF16)
        return carry

    out_copies = []
    for c in range(CHUNKS):
        per_chunk = tiles // CHUNKS
        lax.fori_loop(c * per_chunk, (c + 1) * per_chunk, out_tile, 0, unroll=True)
        cols = pl.ds(c * wide, wide)
        copy = pltpu.make_async_copy(lr_out.at[:, cols], out_h.at[:, cols], out_sem.at[1 + c])
        copy.start()
        out_copies.append(copy)

    for copy in halo:
        @pl.when(jnp.logical_not(last))
        def _():
            copy.wait_send()

    for copy in tp_copies:
        copy.wait_send()
    for (dz, dx), copy in zip(OWNER_STEPS, own_copies):
        if (dz, dx) == (0, 0):
            @pl.when(jnp.logical_not(is_owner))
            def _():
                copy.wait_send()
        else:
            copy.wait_send()

    @pl.when(is_owner)
    def _():
        for d in BLOCK_STEPS:
            @pl.when(block + d < blocks)
            def _():
                total_copy(d, block + d).wait_send()
        for s in range(len(back_steps)):
            pltpu.make_async_copy(carry_out.at[0], carry_out.at[0], back_send.at[s]).wait()

    mixed_copy.wait()
    for copy in out_copies:
        copy.wait()


def per_device(resid, q_mr, k_mr, v_mr, mr_taps, norm_gain, q_lr, k_lr, pole_rate, residue):
    tok, channels = resid.shape
    tp_size = lax.axis_size("tp")
    blocks = lax.axis_size("ctx") // BLOCK
    tiles = channels // LANES
    groups = channels // GROUP
    big = pltpu.VMEM((tok, channels), BF16)
    scratch = [
        big, big, big, big, big, big,
        pltpu.VMEM((groups, TOK), BF16),
        pltpu.VMEM((1, channels), BF16),
        pltpu.VMEM((POLES, groups), F32),
        pltpu.VMEM((POLES, groups), F32),
        pltpu.VMEM((2 * TOK, channels), BF16),
        pltpu.VMEM((groups * TOK, 2 * TOK), BF16),
        pltpu.VMEM((groups * TOK, TOK), BF16),
        pltpu.VMEM((groups * POLES, 2 * TOK), BF16),
        pltpu.VMEM((tiles * TOK, 2 * LANES), BF16),
        pltpu.VMEM((groups, TOK), F32),
        pltpu.VMEM((POLES, groups), F32),
        pltpu.VMEM((groups, TOK), F32),
        big,
        pltpu.VMEM((tok, channels), F32),
        pltpu.VMEM((tok, channels), F32),
        big,
        pltpu.VMEM((tp_size, 8, TOK), F32),
        pltpu.VMEM((OWNERS, 2 * POLES, LANES), BF16),
        pltpu.VMEM((BLOCK, 2 * POLES, LANES), BF16),
        pltpu.VMEM((2 * POLES, LANES), BF16),
        pltpu.VMEM((blocks, 2 * POLES, LANES), BF16),
        pltpu.VMEM((BLOCK, 2 * POLES, LANES), BF16),
        pltpu.VMEM((OWNERS, 2 * POLES, LANES), BF16),
        pltpu.SemaphoreType.DMA((2, CHUNKS)),
        pltpu.SemaphoreType.DMA((8,)),
        pltpu.SemaphoreType.DMA((1 + CHUNKS,)),
        pltpu.SemaphoreType.DMA((CHUNKS,)),
        pltpu.SemaphoreType.DMA((CHUNKS,)),
        pltpu.SemaphoreType.DMA((tp_size,)),
        pltpu.SemaphoreType.DMA((tp_size,)),
        pltpu.SemaphoreType.DMA((OWNERS,)),
        pltpu.SemaphoreType.DMA,
        pltpu.SemaphoreType.DMA((blocks,)),
        pltpu.SemaphoreType.DMA((blocks,)),
        pltpu.SemaphoreType.DMA((2 * OWNERS,)),
        pltpu.SemaphoreType.DMA,
    ]
    anywhere = pl.BlockSpec(memory_space=pl.ANY)
    out = jax.ShapeDtypeStruct((tok, channels), BF16)
    return pl.pallas_call(
        functools.partial(kernel, blocks, tp_size),
        out_shape=(out, out),
        in_specs=[anywhere] * 10,
        out_specs=(anywhere, anywhere),
        scratch_shapes=scratch,
        compiler_params=pltpu.CompilerParams(
            collective_id=0, has_side_effects=True, vmem_limit_bytes=56 * 1024 * 1024
        ),
        name="mixers",
    )(resid, q_mr, k_mr, v_mr, mr_taps, norm_gain.reshape(1, channels), q_lr, k_lr, pole_rate, residue)


def solution(mesh):
    placed = (
        P("ctx", "tp"),
        P("ctx", "tp"),
        P("ctx", "tp"),
        P("ctx", "tp"),
        P("tp", None),
        P("tp"),
        P("ctx", "tp"),
        P("ctx", "tp"),
        P(None, "tp"),
        P(None, "tp"),
    )
    return jax.shard_map(
        per_device,
        mesh=mesh,
        in_specs=placed,
        out_specs=(P("ctx", "tp"), P("ctx", "tp")),
        check_vma=False,
    )
```

time: 657 us -> 46.1 us (0.07)
  the two profiles are of different devices: /device:TPU:487 before, /device:TPU:1 now
where the time goes in v1:
time: 46.1 us; the launch traced here: 45.9 us
  Pallas kernels  41.2 us (89%)
  local copies, waits for them, and re-layouts  4.03 us (9%)
  between operations  0.65 us (1%)
    pallas_call x1, Pallas kernels, per_device(): pl.pallas_call(functools.partial(kernel, blocks, tp_size), out_shape=(out...  41.2 us
    unnamed x4, local copies, waits for them, and re-layouts  2.74 us
    reshape x1, local copies, waits for them, and re-layouts, per_device(): norm_gain.reshape(1, channels)  1.29 us

profile of v1, /device:TPU:1, one launch (start us, length us, event | category | flops | bytes accessed | tf_op | source)
XLA Modules:
  0.0 45.9 jit_solution(10268249343540818765)
XLA Ops:
  0.6 1.3 %reshape.7.gain_h = bf16[1,2048]{1,0:T(2,128)(2,1)} reshape(bf16[2048]{0:T(1024)(128)(2,1)} %param.15) | data formatting | bytes 8192 | tf_op jit(solution)/shard_map/reshape | solution.py:505
  1.9 41.2 %mixers.1 = (bf16[128,2048]{1,0:T(8,128)(2,1)}, bf16[128,2048]{1,0:T(8,128)(2,1)}) custom-call(bf16[128,2048]{1,0:T(8,128)(2,1)} %resid_h.1, bf16[128,2048]{1,0:T(8,128)(2,1)} %q_mr_h.1, bf16[128,2048]{1,0:T(8,128)(2,1)} %k_mr_h.1, bf16[128,2048]{1,0:T(8,128)(2,1)} %v_mr_h.1, bf16[128,128]{1,0:T(8,128)(2,1)} %taps_h.1, bf16[1,2048]{1,0:T(2,128)(2,1)} %reshape.7.gain_h, ...), custom_call_target="tpu_custom_call" | custom-call | tf_op jit(solution)/shard_map/mixers/pallas_call | solution.py:495
  43.1 0.0 copy-start
  43.1 1.9 %copy.14 = bf16[128,2048]{1,0:T(8,128)(2,1)} copy(bf16[128,2048]{1,0:T(8,128)(2,1)} %get-tuple-element.4) | data formatting | bytes 1048576
  45.1 0.0 copy-done
  45.1 0.8 %copy.15 = bf16[128,2048]{1,0:T(8,128)(2,1)} copy(bf16[128,2048]{1,0:T(8,128)(2,1)S(1)} %copy-done) | data formatting | bytes 1048576
Async XLA Ops:
  43.1 2.0 %copy-start = (bf16[128,2048]{1,0:T(8,128)(2,1)S(1)}, bf16[128,2048]{1,0:T(8,128)(2,1)}, u32[]{:S(2)}) copy-start(bf16[128,2048]{1,0:T(8,128)(2,1)} %get-tuple-element.5) | copy-start | bytes 1572868

commit v2 on v1

--- a/solution.py
+++ b/solution.py
@@ -18,7 +18,9 @@
 POLES = 16
 BLOCK = 16
 OWNERS = 8
-CHUNKS = 4
+CHUNKS = (4, 4, 4, 2, 2)
+
+HAND_PIECES = 4
 
 OWNER_STEPS = ((1, 2), (0, 2), (1, 1), (1, 3), (0, 1), (0, 3), (1, 0), (0, 0))
 BLOCK_STEPS = (4, 3, 5, 2, 6, 1, 7)
@@ -37,19 +39,19 @@
     blocks,
     tp_size,
     resid_h, q_mr_h, k_mr_h, v_mr_h, taps_h, gain_h, q_lr_h, k_lr_h, rate_h, residue_h,
-    mixed_h, out_h,
-    k_mr, v_mr, resid, q_mr, k_lr, q_lr, taps, gain, rate, residue,
+    mixed, lr_out,
+    k_mr, v_mr, resid, q_mr, k_lr, q_lr, taps, gain, gain_in, rate, residue,
     window, mr_tab, lr_tab, leave_tab, entry_tab, taps_rev, weight_eff, impulse,
-    mixed, gated, local, lr_out, squares, states, gathered, total, totals, carry_out, carry_in,
-    kv_sem, in_sem, out_sem, halo_send, halo_recv, tp_send, tp_recv,
-    own_send, own_recv, tot_send, tot_recv, back_send, back_recv,
+    gated, local, squares, states, gathered, total, totals, carry_out, carry_in,
+    kv_sem, in_sem, halo_send, halo_recv, tp_send, tp_recv,
+    own_send, own_recv, tot_send, tot_recv, back_send, back_recv, relay,
 ):
     me = lax.axis_index("ctx")
     tp = lax.axis_index("tp")
     shards = blocks * BLOCK
     channels = k_mr.shape[1]
     tiles = channels // LANES
-    wide = channels // CHUNKS
+    starts = [sum(CHUNKS[:c]) for c in range(len(CHUNKS))]
     block = me // BLOCK
     member = me % BLOCK
     base = block * BLOCK
@@ -61,8 +63,8 @@
     is_owner = core == 1
 
     kv_copies = []
-    for c in range(CHUNKS):
-        cols = pl.ds(c * wide, wide)
+    for c in range(len(CHUNKS)):
+        cols = pl.ds(starts[c] * LANES, CHUNKS[c] * LANES)
         pair = []
         for i, (src, dst) in enumerate(((k_mr_h, k_mr), (v_mr_h, v_mr))):
             copy = pltpu.make_async_copy(src.at[:, cols], dst.at[:, cols], kv_sem.at[i, c])
@@ -73,7 +75,7 @@
     for i, (name, src, dst) in enumerate((
         ("taps", taps_h, taps), ("rate", rate_h, rate), ("residue", residue_h, residue),
         ("resid", resid_h, resid), ("q_mr", q_mr_h, q_mr), ("k_lr", k_lr_h, k_lr),
-        ("gain", gain_h, gain), ("q_lr", q_lr_h, q_lr),
+        ("gain", gain_h, gain_in), ("q_lr", q_lr_h, q_lr),
     )):
         in_copies[name] = pltpu.make_async_copy(src, dst, in_sem.at[i])
         in_copies[name].start()
@@ -105,22 +107,22 @@
         for dz, dx in OWNER_STEPS:
             chip = base + ((z_at + dz) % 2) * 8 + ((x_at + dx) % 4) * 2
             greet(chip, tp)
-        for d in range(1, blocks):
-            greet(((block + d) % blocks) * BLOCK + member, tp)
+        greet(((block + 1) % blocks) * BLOCK + member, tp)
+        greet(((block + blocks - 1) % blocks) * BLOCK + member, tp)
 
     @pl.when(jnp.logical_not(is_owner))
     def _():
         greet(me + 1, tp)
 
     halo = []
-    for c in range(CHUNKS):
+    for c in range(len(CHUNKS)):
         for copy in kv_copies[c]:
             copy.wait()
-        cols = pl.ds(c * wide, wide)
+        cols = pl.ds(starts[c] * LANES, CHUNKS[c] * LANES)
         window[TOK:, cols] = (k_mr[:, cols].astype(F32) * v_mr[:, cols].astype(F32)).astype(BF16)
         if c == 0:
             ends = jnp.where(first, 0, 1) + jnp.where(last, 0, 1)
-            near = jnp.where(is_owner, BLOCK - 1 + blocks - 1, OWNERS)
+            near = jnp.where(is_owner, BLOCK - 1 + 2, OWNERS)
             pl.semaphore_wait(barrier, ends + near + (tp_size - 1))
 
         copy = pltpu.make_async_remote_copy(
@@ -141,6 +143,22 @@
     def _():
         window[:TOK, :] = jnp.zeros((TOK, channels), BF16)
 
+    def pass_on(step):
+        @pl.when(is_owner)
+        def _():
+            for d in (step, blocks - step):
+                pl.semaphore_signal(
+                    relay.at[step - 1], inc=1,
+                    device_id=(((block + d) % blocks) * BLOCK + member, tp), device_id_type=MESH,
+                )
+
+    def hear(step):
+        @pl.when(is_owner)
+        def _():
+            pl.semaphore_wait(relay.at[step - 1], 2)
+
+    pass_on(1)
+
     row_of = lax.broadcasted_iota(jnp.int32, (TOK, TOK), 0)
     col_of = lax.broadcasted_iota(jnp.int32, (TOK, TOK), 1)
     diagonal = row_of == col_of
@@ -178,7 +196,8 @@
         rows = pl.ds(pl.multiple_of(j * TOK, TOK), TOK)
         high = leave.astype(BF16)
         leave_tab[rows, :TOK] = high
-        leave_tab[rows, TOK:] = (leave - high.astype(F32)).astype(BF16)
+        leave_tab[rows, TOK : 2 * TOK] = (leave - high.astype(F32)).astype(BF16)
+        leave_tab[rows, 2 * TOK :] = high
         weighted = of_rows(j, weights) * leave
         lines = [
             jnp.sum(weighted[i * POLES : (i + 1) * POLES], axis=0, keepdims=True)
@@ -196,7 +215,11 @@
             line = jnp.broadcast_to(impulse[pl.ds(g, 1), :], (TOK, TOK))
             square = pltpu.roll(line, 0, 1, stride=1, stride_axis=0)
             rows = pl.ds(pl.multiple_of(g * TOK, TOK), TOK)
-            lr_tab[rows, :] = jnp.where(causal, square, 0.0).astype(BF16)
+            square = jnp.where(causal, square, 0.0)
+            high = square.astype(BF16)
+            lr_tab[rows, :TOK] = high
+            lr_tab[rows, TOK : 2 * TOK] = (square - high.astype(F32)).astype(BF16)
+            lr_tab[rows, 2 * TOK :] = high
         return carry
 
     def entry_table(j, carry):
@@ -214,10 +237,13 @@
             out = jnp.where(mask == i, stacked[i * rows : (i + 1) * rows], out)
         return out
 
+    hear(1)
+    pass_on(2)
+
     squares_sum = jnp.zeros((TOK, LANES), F32)
     for name in ("resid", "q_mr"):
         in_copies[name].wait()
-    for c in range(CHUNKS):
+    for c in range(len(CHUNKS)):
         @pl.when(jnp.logical_not(first))
         def _():
             halo[c].wait_recv()
@@ -232,8 +258,7 @@
             result = result.astype(F32)
             return acc + result * result
 
-        per_chunk = tiles // CHUNKS
-        squares_sum = lax.fori_loop(c * per_chunk, (c + 1) * per_chunk, mr_tile, squares_sum, unroll=True)
+        squares_sum = lax.fori_loop(starts[c], starts[c] + CHUNKS[c], mr_tile, squares_sum, unroll=True)
 
     row_sum = jnp.sum(squares_sum, axis=1, keepdims=True)
     line = jnp.sum(jnp.where(diagonal, row_sum, 0.0), axis=0, keepdims=True)
@@ -250,20 +275,19 @@
         )
         copy.start()
         tp_copies.append(copy)
-    mixed_copy = pltpu.make_async_copy(mixed, mixed_h, out_sem.at[0])
-    mixed_copy.start()
     for name in ("k_lr", "gain", "q_lr"):
         in_copies[name].wait()
 
+    gain[...] = gain_in[...].astype(F32)
+
     def gate_tile(j, carry):
         cols = pl.ds(pl.multiple_of(j * LANES, LANES), LANES)
-        scaled = mixed[:, cols].astype(F32) * gain[:, cols].astype(F32)
+        scaled = mixed[:, cols].astype(F32) * gain[pl.ds(j, 1), :]
         gated[:, cols] = scaled * k_lr[:, cols].astype(F32)
         return carry
 
     lax.fori_loop(0, tiles, gate_tile, 0, unroll=4)
     lax.fori_loop(0, tiles, lr_tables, 0, unroll=4)
-    lax.fori_loop(0, tiles, entry_table, 0, unroll=4)
     for copy in tp_copies:
         copy.wait_recv()
     line = squares[0, :1, :]
@@ -274,6 +298,11 @@
 
     lr_in = window
 
+    for copy in halo:
+        @pl.when(jnp.logical_not(last))
+        def _():
+            copy.wait_send()
+
     own_copies = []
     for s, (dz, dx) in enumerate(OWNER_STEPS):
         z_to, x_to = (z_at + dz) % 2, (x_at + dx) % 4
@@ -281,11 +310,16 @@
         for half in range(2):
             j = owner * 2 + half
             cols = pl.ds(pl.multiple_of(j * LANES, LANES), LANES)
-            value = (gated[:, cols] * scale).astype(BF16)
-            lr_in[:TOK, cols] = value
+            value = gated[:, cols] * scale
+            high = value.astype(BF16)
+            low = (value - high.astype(F32)).astype(BF16)
+            lr_in[:TOK, cols] = high
+            lr_in[TOK:, cols] = low
             rows = pl.ds(pl.multiple_of(j * LANES, LANES), LANES)
             stacked = jnp.dot(
-                leave_tab[rows, :], jnp.concatenate([value, value], axis=0), preferred_element_type=F32
+                leave_tab[rows, :],
+                jnp.concatenate([high, high, low], axis=0),
+                preferred_element_type=F32,
             )
             states[s, half * POLES : (half + 1) * POLES, :] = own_lanes(stacked, POLES).astype(BF16)
         copy = pltpu.make_async_remote_copy(
@@ -314,11 +348,16 @@
     def lr_conv_tile(j, carry):
         cols = pl.ds(pl.multiple_of(j * LANES, LANES), LANES)
         rows = pl.ds(pl.multiple_of(j * PER_TILE * TOK, TOK), PER_TILE * TOK)
-        stacked = jnp.dot(lr_tab[rows, :], lr_in[:TOK, cols], preferred_element_type=F32)
+        high, low = lr_in[:TOK, cols], lr_in[TOK:, cols]
+        stacked = jnp.dot(
+            lr_tab[rows, :], jnp.concatenate([high, high, low], axis=0), preferred_element_type=F32
+        )
         local[:, cols] = own_lanes(stacked, TOK)
         return carry
 
     lax.fori_loop(0, tiles // 2, lr_conv_tile, 0, unroll=4)
+
+    hear(2)
 
     my_owner = z_at * 4 + x_at
 
@@ -359,6 +398,7 @@
                 total_copy(d, block + d).start()
 
         lax.fori_loop(tiles // 2, tiles, lr_conv_tile, 0, unroll=4)
+        lax.fori_loop(0, tiles, entry_table, 0, unroll=4)
 
         carried = jnp.zeros((2 * POLES, LANES), F32)
         for b in range(blocks - 1):
@@ -390,6 +430,7 @@
     @pl.when(jnp.logical_not(is_owner))
     def _():
         lax.fori_loop(tiles // 2, tiles, lr_conv_tile, 0, unroll=4)
+        lax.fori_loop(0, tiles, entry_table, 0, unroll=4)
         pltpu.make_async_copy(carry_in, carry_in, back_recv).wait()
 
     lane_group = lax.broadcasted_iota(jnp.int32, (POLES, LANES), 1) // GROUP
@@ -406,19 +447,7 @@
         lr_out[:, cols] = (q_lr[:, cols].astype(F32) * conv).astype(BF16)
         return carry
 
-    out_copies = []
-    for c in range(CHUNKS):
-        per_chunk = tiles // CHUNKS
-        lax.fori_loop(c * per_chunk, (c + 1) * per_chunk, out_tile, 0, unroll=True)
-        cols = pl.ds(c * wide, wide)
-        copy = pltpu.make_async_copy(lr_out.at[:, cols], out_h.at[:, cols], out_sem.at[1 + c])
-        copy.start()
-        out_copies.append(copy)
-
-    for copy in halo:
-        @pl.when(jnp.logical_not(last))
-        def _():
-            copy.wait_send()
+    lax.fori_loop(0, tiles, out_tile, 0, unroll=True)
 
     for copy in tp_copies:
         copy.wait_send()
@@ -439,8 +468,17 @@
         for s in range(len(back_steps)):
             pltpu.make_async_copy(carry_out.at[0], carry_out.at[0], back_send.at[s]).wait()
 
-    mixed_copy.wait()
-    for copy in out_copies:
+
+def hand_over(mixed, lr_out, mixed_to, lr_out_to, sems):
+    rows = TOK // HAND_PIECES
+    copies = []
+    for i, (src, dst) in enumerate(((mixed, mixed_to), (lr_out, lr_out_to))):
+        for c in range(HAND_PIECES):
+            part = pl.ds(c * rows, rows)
+            copies.append(pltpu.make_async_copy(src.at[part], dst.at[part], sems.at[i, c]))
+    for copy in copies:
+        copy.start()
+    for copy in copies:
         copy.wait()
 
 
@@ -454,21 +492,20 @@
     scratch = [
         big, big, big, big, big, big,
         pltpu.VMEM((groups, TOK), BF16),
-        pltpu.VMEM((1, channels), BF16),
+        pltpu.VMEM((tiles, LANES), F32),
+        pltpu.VMEM((tiles, LANES), BF16),
         pltpu.VMEM((POLES, groups), F32),
         pltpu.VMEM((POLES, groups), F32),
         pltpu.VMEM((2 * TOK, channels), BF16),
         pltpu.VMEM((groups * TOK, 2 * TOK), BF16),
-        pltpu.VMEM((groups * TOK, TOK), BF16),
-        pltpu.VMEM((groups * POLES, 2 * TOK), BF16),
+        pltpu.VMEM((groups * TOK, 3 * TOK), BF16),
+        pltpu.VMEM((groups * POLES, 3 * TOK), BF16),
         pltpu.VMEM((tiles * TOK, 2 * LANES), BF16),
         pltpu.VMEM((groups, TOK), F32),
         pltpu.VMEM((POLES, groups), F32),
         pltpu.VMEM((groups, TOK), F32),
-        big,
         pltpu.VMEM((tok, channels), F32),
         pltpu.VMEM((tok, channels), F32),
-        big,
         pltpu.VMEM((tp_size, 8, TOK), F32),
         pltpu.VMEM((OWNERS, 2 * POLES, LANES), BF16),
         pltpu.VMEM((BLOCK, 2 * POLES, LANES), BF16),
@@ -476,11 +513,10 @@
         pltpu.VMEM((blocks, 2 * POLES, LANES), BF16),
         pltpu.VMEM((BLOCK, 2 * POLES, LANES), BF16),
         pltpu.VMEM((OWNERS, 2 * POLES, LANES), BF16),
-        pltpu.SemaphoreType.DMA((2, CHUNKS)),
+        pltpu.SemaphoreType.DMA((2, len(CHUNKS))),
         pltpu.SemaphoreType.DMA((8,)),
-        pltpu.SemaphoreType.DMA((1 + CHUNKS,)),
-        pltpu.SemaphoreType.DMA((CHUNKS,)),
-        pltpu.SemaphoreType.DMA((CHUNKS,)),
+        pltpu.SemaphoreType.DMA((len(CHUNKS),)),
+        pltpu.SemaphoreType.DMA((len(CHUNKS),)),
         pltpu.SemaphoreType.DMA((tp_size,)),
         pltpu.SemaphoreType.DMA((tp_size,)),
         pltpu.SemaphoreType.DMA((OWNERS,)),
@@ -489,20 +525,29 @@
         pltpu.SemaphoreType.DMA((blocks,)),
         pltpu.SemaphoreType.DMA((2 * OWNERS,)),
         pltpu.SemaphoreType.DMA,
+        pltpu.SemaphoreType.REGULAR((2,)),
     ]
-    anywhere = pl.BlockSpec(memory_space=pl.ANY)
+    in_place = pl.BlockSpec(memory_space=pl.ANY)
     out = jax.ShapeDtypeStruct((tok, channels), BF16)
-    return pl.pallas_call(
+    results = pl.pallas_call(
         functools.partial(kernel, blocks, tp_size),
         out_shape=(out, out),
-        in_specs=[anywhere] * 10,
-        out_specs=(anywhere, anywhere),
+        in_specs=[in_place] * 10,
+        out_specs=(pl.BlockSpec(memory_space=pltpu.VMEM),) * 2,
         scratch_shapes=scratch,
         compiler_params=pltpu.CompilerParams(
             collective_id=0, has_side_effects=True, vmem_limit_bytes=56 * 1024 * 1024
         ),
         name="mixers",
-    )(resid, q_mr, k_mr, v_mr, mr_taps, norm_gain.reshape(1, channels), q_lr, k_lr, pole_rate, residue)
+    )(resid, q_mr, k_mr, v_mr, mr_taps, norm_gain.reshape(tiles, LANES), q_lr, k_lr, pole_rate, residue)
+    return pl.pallas_call(
+        hand_over,
+        out_shape=(out, out),
+        in_specs=[in_place] * 2,
+        out_specs=(in_place, in_place),
+        scratch_shapes=[pltpu.SemaphoreType.DMA((2, HAND_PIECES))],
+        name="hand_over",
+    )(*results)
 
 
 def solution(mesh):

time: 46.1 us -> 73.4 us (1.59)
  Pallas kernels: 41.2 us -> 72.6 us
  local copies, waits for them, and re-layouts: 4.03 us -> 0 us
    pallas_call x0 -> x1, Pallas kernels: none -> 32.9 us  [per_device(): pl.pallas_call(hand_over, out_shape=(out, out), in_specs=[in_place] * 2,...]
    unnamed x4 -> x0, local copies, waits for them, and re-layouts: 2.74 us -> none
    pallas_call x1, Pallas kernels: 41.2 us -> 39.7 us  [per_device(): pl.pallas_call(functools.partial(kernel, blocks, tp_size), out_shape=(out...]
    reshape x1 -> x0, local copies, waits for them, and re-layouts: 1.29 us -> none  [per_device(): norm_gain.reshape(1, channels)]
where the time goes in v2:
time: 73.4 us; the launch traced here: 73.3 us
  Pallas kernels  72.6 us (99%)
    pallas_call x1, Pallas kernels, per_device(): pl.pallas_call(functools.partial(kernel, blocks, tp_size), out_shape=(out...  39.7 us
    pallas_call x1, Pallas kernels, per_device(): pl.pallas_call(hand_over, out_shape=(out, out), in_specs=[in_place] * 2,...  32.9 us

profile of v2, /device:TPU:1, one launch (start us, length us, event | category | flops | bytes accessed | tf_op | source)
XLA Modules:
  0.0 73.3 jit_solution(13924226772985282947)
XLA Ops:
  0.6 39.7 %mixers.1 = (bf16[128,2048]{1,0:T(8,128)(2,1)}, bf16[128,2048]{1,0:T(8,128)(2,1)}) custom-call(bf16[128,2048]{1,0:T(8,128)(2,1)} %resid_h.1, bf16[128,2048]{1,0:T(8,128)(2,1)} %q_mr_h.1, bf16[128,2048]{1,0:T(8,128)(2,1)} %k_mr_h.1, bf16[128,2048]{1,0:T(8,128)(2,1)} %v_mr_h.1, bf16[128,128]{1,0:T(8,128)(2,1)} %taps_h.1, bf16[16,128]{1,0:T(8,128)(2,1)} %bitcast.1, ...), custom_call_target="tpu_custom_call" | custom-call | tf_op jit(solution)/shard_map/mixers/pallas_call | solution.py:532
  40.4 32.9 %hand_over.1 = (bf16[128,2048]{1,0:T(8,128)(2,1)}, bf16[128,2048]{1,0:T(8,128)(2,1)}) custom-call(bf16[128,2048]{1,0:T(8,128)(2,1)} %get-tuple-element.4.mixed, bf16[128,2048]{1,0:T(8,128)(2,1)} %get-tuple-element.5.lr_out), custom_call_target="tpu_custom_call" | custom-call | tf_op jit(solution)/shard_map/hand_over/pallas_call | solution.py:543

commit v3 on v2

--- a/solution.py
+++ b/solution.py
@@ -39,11 +39,11 @@
     blocks,
     tp_size,
     resid_h, q_mr_h, k_mr_h, v_mr_h, taps_h, gain_h, q_lr_h, k_lr_h, rate_h, residue_h,
-    mixed, lr_out,
+    mixed_h, out_h,
     k_mr, v_mr, resid, q_mr, k_lr, q_lr, taps, gain, gain_in, rate, residue,
     window, mr_tab, lr_tab, leave_tab, entry_tab, taps_rev, weight_eff, impulse,
-    gated, local, squares, states, gathered, total, totals, carry_out, carry_in,
-    kv_sem, in_sem, halo_send, halo_recv, tp_send, tp_recv,
+    mixed, gated, local, lr_out, squares, states, gathered, total, totals, carry_out, carry_in,
+    kv_sem, in_sem, out_sem, halo_send, halo_recv, tp_send, tp_recv,
     own_send, own_recv, tot_send, tot_recv, back_send, back_recv, relay,
 ):
     me = lax.axis_index("ctx")
@@ -207,8 +207,6 @@
         impulse[rows, :] = pltpu.roll(jnp.concatenate(lines, axis=0), 1, 1)
         return carry
 
-    lax.fori_loop(0, tiles, leave_table, 0, unroll=4)
-
     def lr_tables(j, carry):
         for i in range(PER_TILE):
             g = j * PER_TILE + i
@@ -275,6 +273,8 @@
         )
         copy.start()
         tp_copies.append(copy)
+    mixed_copy = pltpu.make_async_copy(mixed, mixed_h, out_sem.at[0])
+    mixed_copy.start()
     for name in ("k_lr", "gain", "q_lr"):
         in_copies[name].wait()
 
@@ -286,8 +286,8 @@
         gated[:, cols] = scaled * k_lr[:, cols].astype(F32)
         return carry
 
+    lax.fori_loop(0, tiles, leave_table, 0, unroll=4)
     lax.fori_loop(0, tiles, gate_tile, 0, unroll=4)
-    lax.fori_loop(0, tiles, lr_tables, 0, unroll=4)
     for copy in tp_copies:
         copy.wait_recv()
     line = squares[0, :1, :]
@@ -355,7 +355,7 @@
         local[:, cols] = own_lanes(stacked, TOK)
         return carry
 
-    lax.fori_loop(0, tiles // 2, lr_conv_tile, 0, unroll=4)
+    lax.fori_loop(0, tiles, lr_tables, 0, unroll=4)
 
     hear(2)
 
@@ -397,7 +397,7 @@
             def _():
                 total_copy(d, block + d).start()
 
-        lax.fori_loop(tiles // 2, tiles, lr_conv_tile, 0, unroll=4)
+        lax.fori_loop(0, tiles, lr_conv_tile, 0, unroll=4)
         lax.fori_loop(0, tiles, entry_table, 0, unroll=4)
 
         carried = jnp.zeros((2 * POLES, LANES), F32)
@@ -418,36 +418,47 @@
                 src_ref=carry_out.at[to],
                 dst_ref=carry_in.at[my_owner],
                 send_sem=back_send.at[s],
-                recv_sem=back_recv,
+                recv_sem=back_recv.at[my_owner],
                 device_id=(base + to, tp),
                 device_id_type=MESH,
             ).start()
         carry_in[my_owner] = carry_out[member]
-        pltpu.make_async_copy(
-            carry_in.at[pl.ds(0, OWNERS - 1)], carry_in.at[pl.ds(0, OWNERS - 1)], back_recv
-        ).wait()
 
     @pl.when(jnp.logical_not(is_owner))
     def _():
-        lax.fori_loop(tiles // 2, tiles, lr_conv_tile, 0, unroll=4)
+        lax.fori_loop(0, tiles, lr_conv_tile, 0, unroll=4)
         lax.fori_loop(0, tiles, entry_table, 0, unroll=4)
-        pltpu.make_async_copy(carry_in, carry_in, back_recv).wait()
 
     lane_group = lax.broadcasted_iota(jnp.int32, (POLES, LANES), 1) // GROUP
     pole_masks = [(lane_group == i).astype(F32).astype(BF16) for i in range(PER_TILE)]
 
-    def out_tile(j, carry):
-        cols = pl.ds(pl.multiple_of(j * LANES, LANES), LANES)
-        rows = pl.ds(pl.multiple_of(j * TOK, TOK), TOK)
-        came = carry_in[j // 2, pl.ds(pl.multiple_of((j % 2) * POLES, POLES), POLES), :]
+    def out_tile(owner, half):
+        cols = pl.ds(pl.multiple_of((owner * 2 + half) * LANES, LANES), LANES)
+        rows = pl.ds(pl.multiple_of((owner * 2 + half) * TOK, TOK), TOK)
+        came = carry_in[owner, half * POLES : (half + 1) * POLES, :]
         spread = [came * mask for mask in pole_masks]
         spread = jnp.concatenate(spread + spread, axis=0)
         incoming = jnp.dot(entry_tab[rows, :], spread, preferred_element_type=F32)
         conv = local[:, cols] + incoming
         lr_out[:, cols] = (q_lr[:, cols].astype(F32) * conv).astype(BF16)
-        return carry
-
-    lax.fori_loop(0, tiles, out_tile, 0, unroll=True)
+
+    out_copies = []
+    for s, (dz, dx) in enumerate(reversed(OWNER_STEPS)):
+        owner = ((z_at + dz) % 2) * 4 + (x_at + dx) % 4
+
+        def arrive():
+            pltpu.make_async_copy(carry_in.at[owner], carry_in.at[owner], back_recv.at[owner]).wait()
+
+        if (dz, dx) == (0, 0):
+            pl.when(jnp.logical_not(is_owner))(arrive)
+        else:
+            arrive()
+        for half in range(2):
+            out_tile(owner, half)
+        cols = pl.ds(pl.multiple_of(owner * 2 * LANES, 2 * LANES), 2 * LANES)
+        copy = pltpu.make_async_copy(lr_out.at[:, cols], out_h.at[:, cols], out_sem.at[1 + s])
+        copy.start()
+        out_copies.append(copy)
 
     for copy in tp_copies:
         copy.wait_send()
@@ -468,17 +479,25 @@
         for s in range(len(back_steps)):
             pltpu.make_async_copy(carry_out.at[0], carry_out.at[0], back_send.at[s]).wait()
 
-
-def hand_over(mixed, lr_out, mixed_to, lr_out_to, sems):
+    mixed_copy.wait()
+    for copy in out_copies:
+        copy.wait()
+
+
+def hand_over(mixed, lr_out, mixed_to, lr_out_to, held, in_sems, out_sems):
     rows = TOK // HAND_PIECES
-    copies = []
-    for i, (src, dst) in enumerate(((mixed, mixed_to), (lr_out, lr_out_to))):
-        for c in range(HAND_PIECES):
-            part = pl.ds(c * rows, rows)
-            copies.append(pltpu.make_async_copy(src.at[part], dst.at[part], sems.at[i, c]))
-    for copy in copies:
+    inward, outward = [], []
+    for c in range(HAND_PIECES):
+        part = pl.ds(c * rows, rows)
+        for i, (src, dst) in enumerate(((mixed, mixed_to), (lr_out, lr_out_to))):
+            inward.append(pltpu.make_async_copy(src.at[part], held.at[i, part], in_sems.at[i, c]))
+            outward.append(pltpu.make_async_copy(held.at[i, part], dst.at[part], out_sems.at[i, c]))
+    for copy in inward:
         copy.start()
-    for copy in copies:
+    for came, copy in zip(inward, outward):
+        came.wait()
+        copy.start()
+    for copy in outward:
         copy.wait()
 
 
@@ -504,8 +523,10 @@
         pltpu.VMEM((groups, TOK), F32),
         pltpu.VMEM((POLES, groups), F32),
         pltpu.VMEM((groups, TOK), F32),
+        big,
         pltpu.VMEM((tok, channels), F32),
         pltpu.VMEM((tok, channels), F32),
+        big,
         pltpu.VMEM((tp_size, 8, TOK), F32),
         pltpu.VMEM((OWNERS, 2 * POLES, LANES), BF16),
         pltpu.VMEM((BLOCK, 2 * POLES, LANES), BF16),
@@ -515,6 +536,7 @@
         pltpu.VMEM((OWNERS, 2 * POLES, LANES), BF16),
         pltpu.SemaphoreType.DMA((2, len(CHUNKS))),
         pltpu.SemaphoreType.DMA((8,)),
+        pltpu.SemaphoreType.DMA((1 + OWNERS,)),
         pltpu.SemaphoreType.DMA((len(CHUNKS),)),
         pltpu.SemaphoreType.DMA((len(CHUNKS),)),
         pltpu.SemaphoreType.DMA((tp_size,)),
@@ -524,7 +546,7 @@
         pltpu.SemaphoreType.DMA((blocks,)),
         pltpu.SemaphoreType.DMA((blocks,)),
         pltpu.SemaphoreType.DMA((2 * OWNERS,)),
-        pltpu.SemaphoreType.DMA,
+        pltpu.SemaphoreType.DMA((OWNERS,)),
         pltpu.SemaphoreType.REGULAR((2,)),
     ]
     in_place = pl.BlockSpec(memory_space=pl.ANY)
@@ -533,7 +555,7 @@
         functools.partial(kernel, blocks, tp_size),
         out_shape=(out, out),
         in_specs=[in_place] * 10,
-        out_specs=(pl.BlockSpec(memory_space=pltpu.VMEM),) * 2,
+        out_specs=(in_place, in_place),
         scratch_shapes=scratch,
         compiler_params=pltpu.CompilerParams(
             collective_id=0, has_side_effects=True, vmem_limit_bytes=56 * 1024 * 1024
@@ -545,7 +567,12 @@
         out_shape=(out, out),
         in_specs=[in_place] * 2,
         out_specs=(in_place, in_place),
-        scratch_shapes=[pltpu.SemaphoreType.DMA((2, HAND_PIECES))],
+        scratch_shapes=[
+            pltpu.VMEM((2, tok, channels), BF16),
+            pltpu.SemaphoreType.DMA((2, HAND_PIECES)),
+            pltpu.SemaphoreType.DMA((2, HAND_PIECES)),
+        ],
+        compiler_params=pltpu.CompilerParams(vmem_limit_bytes=56 * 1024 * 1024),
         name="hand_over",
     )(*results)
 

time: 73.4 us -> 44.6 us (0.61)
  Pallas kernels: 72.6 us -> 43.8 us
    pallas_call x1, Pallas kernels: 32.9 us -> 2.09 us  [per_device(): pl.pallas_call(hand_over, out_shape=(out, out), in_specs=[in_place] * 2,...]
    pallas_call x1, Pallas kernels: 39.7 us -> 41.7 us  [per_device(): pl.pallas_call(functools.partial(kernel, blocks, tp_size), out_shape=(out...]
where the time goes in v3:
time: 44.6 us; the launch traced here: 44.5 us
  Pallas kernels  43.8 us (98%)
  between operations  0.64 us (1%)
    pallas_call x1, Pallas kernels, per_device(): pl.pallas_call(functools.partial(kernel, blocks, tp_size), out_shape=(out...  41.7 us
    pallas_call x1, Pallas kernels, per_device(): pl.pallas_call(hand_over, out_shape=(out, out), in_specs=[in_place] * 2,...  2.09 us

profile of v3, /device:TPU:1, one launch (start us, length us, event | category | flops | bytes accessed | tf_op | source)
XLA Modules:
  0.0 44.5 jit_solution(11116502853580379271)
XLA Ops:
  0.6 41.7 %mixers.1 = (bf16[128,2048]{1,0:T(8,128)(2,1)}, bf16[128,2048]{1,0:T(8,128)(2,1)}) custom-call(bf16[128,2048]{1,0:T(8,128)(2,1)} %resid_h.1, bf16[128,2048]{1,0:T(8,128)(2,1)} %q_mr_h.1, bf16[128,2048]{1,0:T(8,128)(2,1)} %k_mr_h.1, bf16[128,2048]{1,0:T(8,128)(2,1)} %v_mr_h.1, bf16[128,128]{1,0:T(8,128)(2,1)} %taps_h.1, bf16[16,128]{1,0:T(8,128)(2,1)} %bitcast.1, ...), custom_call_target="tpu_custom_call" | custom-call | tf_op jit(solution)/shard_map/mixers/pallas_call | solution.py:554
  42.4 2.1 %hand_over.1 = (bf16[128,2048]{1,0:T(8,128)(2,1)}, bf16[128,2048]{1,0:T(8,128)(2,1)}) custom-call(bf16[128,2048]{1,0:T(8,128)(2,1)} %get-tuple-element.4.mixed, bf16[128,2048]{1,0:T(8,128)(2,1)} %get-tuple-element.5.lr_out), custom_call_target="tpu_custom_call" | custom-call | tf_op jit(solution)/shard_map/hand_over/pallas_call | solution.py:565

commit v4 on v3

--- a/solution.py
+++ b/solution.py
@@ -20,7 +20,9 @@
 OWNERS = 8
 CHUNKS = (4, 4, 4, 2, 2)
 
-HAND_PIECES = 4
+TWO_TP, ROUND_1, ROUND_2, ROUND_3, ALL_OWNERS, BLOCKS_1, BLOCKS_2 = range(7)
+
+HAND_PIECES = 8
 
 OWNER_STEPS = ((1, 2), (0, 2), (1, 1), (1, 3), (0, 1), (0, 3), (1, 0), (0, 0))
 BLOCK_STEPS = (4, 3, 5, 2, 6, 1, 7)
@@ -62,6 +64,34 @@
     last = me == shards - 1
     is_owner = core == 1
 
+    totals[...] = jnp.zeros_like(totals)
+
+    barrier = pltpu.get_barrier_semaphore()
+
+    def greet(ctx, tp_to):
+        pl.semaphore_signal(barrier, inc=1, device_id=(ctx, tp_to), device_id_type=MESH)
+
+    @pl.when(jnp.logical_not(last))
+    def _():
+        greet(me + 1, tp)
+
+    @pl.when(jnp.logical_not(first))
+    def _():
+        greet(me - 1, tp)
+
+    for d in (1, tp_size - 1):
+        greet(me, (tp + d) % tp_size)
+    plane = me // 8
+    planes = shards // 8
+    beside = [plane * 8 + ((x_at + d) % 4) * 2 + core for d in (1, 3)]
+    above = [((plane + d) % planes) * 8 + x_at * 2 + core for d in (1, planes - 1)]
+    partner = base + (1 - z_at) * 8 + x_at * 2 + core
+
+    @pl.when(is_owner)
+    def _():
+        for to in beside + above:
+            greet(to, tp)
+
     kv_copies = []
     for c in range(len(CHUNKS)):
         cols = pl.ds(starts[c] * LANES, CHUNKS[c] * LANES)
@@ -71,49 +101,6 @@
             copy.start()
             pair.append(copy)
         kv_copies.append(pair)
-    in_copies = {}
-    for i, (name, src, dst) in enumerate((
-        ("taps", taps_h, taps), ("rate", rate_h, rate), ("residue", residue_h, residue),
-        ("resid", resid_h, resid), ("q_mr", q_mr_h, q_mr), ("k_lr", k_lr_h, k_lr),
-        ("gain", gain_h, gain_in), ("q_lr", q_lr_h, q_lr),
-    )):
-        in_copies[name] = pltpu.make_async_copy(src, dst, in_sem.at[i])
-        in_copies[name].start()
-
-    totals[...] = jnp.zeros_like(totals)
-
-    barrier = pltpu.get_barrier_semaphore()
-
-    def greet(ctx, tp_to):
-        pl.semaphore_signal(barrier, inc=1, device_id=(ctx, tp_to), device_id_type=MESH)
-
-    @pl.when(jnp.logical_not(last))
-    def _():
-        greet(me + 1, tp)
-
-    @pl.when(jnp.logical_not(first))
-    def _():
-        greet(me - 1, tp)
-
-    for d in range(1, tp_size):
-        greet(me, (tp + d) % tp_size)
-    for dz, dx in OWNER_STEPS:
-        chip = base + ((z_at + dz) % 2) * 8 + ((x_at + dx) % 4) * 2
-        if (dz, dx) != (0, 0):
-            greet(chip + 1, tp)
-
-    @pl.when(is_owner)
-    def _():
-        for dz, dx in OWNER_STEPS:
-            chip = base + ((z_at + dz) % 2) * 8 + ((x_at + dx) % 4) * 2
-            greet(chip, tp)
-        greet(((block + 1) % blocks) * BLOCK + member, tp)
-        greet(((block + blocks - 1) % blocks) * BLOCK + member, tp)
-
-    @pl.when(jnp.logical_not(is_owner))
-    def _():
-        greet(me + 1, tp)
-
     halo = []
     for c in range(len(CHUNKS)):
         for copy in kv_copies[c]:
@@ -122,8 +109,8 @@
         window[TOK:, cols] = (k_mr[:, cols].astype(F32) * v_mr[:, cols].astype(F32)).astype(BF16)
         if c == 0:
             ends = jnp.where(first, 0, 1) + jnp.where(last, 0, 1)
-            near = jnp.where(is_owner, BLOCK - 1 + 2, OWNERS)
-            pl.semaphore_wait(barrier, ends + near + (tp_size - 1))
+            near = jnp.where(is_owner, 2 + 4, 2)
+            pl.semaphore_wait(barrier, ends + near)
 
         copy = pltpu.make_async_remote_copy(
             src_ref=window.at[pl.ds(TOK, TOK), cols],
@@ -143,21 +130,30 @@
     def _():
         window[:TOK, :] = jnp.zeros((TOK, channels), BF16)
 
-    def pass_on(step):
-        @pl.when(is_owner)
-        def _():
-            for d in (step, blocks - step):
-                pl.semaphore_signal(
-                    relay.at[step - 1], inc=1,
-                    device_id=(((block + d) % blocks) * BLOCK + member, tp), device_id_type=MESH,
-                )
-
-    def hear(step):
-        @pl.when(is_owner)
-        def _():
-            pl.semaphore_wait(relay.at[step - 1], 2)
-
-    pass_on(1)
+    def tell(word, to, to_tp):
+        pl.semaphore_signal(
+            relay.at[word], inc=1, device_id=(to, to_tp), device_id_type=MESH
+        )
+
+    def tell_blocks(word, step):
+        for d in (step, blocks - step):
+            tell(word, ((block + d) % blocks) * BLOCK + member, tp)
+
+    tell(TWO_TP, me, (tp + 1) % tp_size)
+
+    @pl.when(is_owner)
+    def _():
+        for to in beside + above:
+            tell(ROUND_1, to, tp)
+
+    in_copies = {}
+    for i, (name, src, dst) in enumerate((
+        ("taps", taps_h, taps), ("rate", rate_h, rate), ("residue", residue_h, residue),
+        ("resid", resid_h, resid), ("q_mr", q_mr_h, q_mr), ("k_lr", k_lr_h, k_lr),
+        ("gain", gain_h, gain_in), ("q_lr", q_lr_h, q_lr),
+    )):
+        in_copies[name] = pltpu.make_async_copy(src, dst, in_sem.at[i])
+        in_copies[name].start()
 
     row_of = lax.broadcasted_iota(jnp.int32, (TOK, TOK), 0)
     col_of = lax.broadcasted_iota(jnp.int32, (TOK, TOK), 1)
@@ -235,8 +231,12 @@
             out = jnp.where(mask == i, stacked[i * rows : (i + 1) * rows], out)
         return out
 
-    hear(1)
-    pass_on(2)
+    @pl.when(is_owner)
+    def _():
+        pl.semaphore_wait(relay.at[ROUND_1], 4)
+        for to in beside + [partner]:
+            tell(ROUND_2, to, tp)
+        tell_blocks(BLOCKS_1, 1)
 
     squares_sum = jnp.zeros((TOK, LANES), F32)
     for name in ("resid", "q_mr"):
@@ -256,11 +256,22 @@
             result = result.astype(F32)
             return acc + result * result
 
+        if c == 2:
+            @pl.when(is_owner)
+            def _():
+                pl.semaphore_wait(relay.at[ROUND_2], 3)
+                for to in beside + [partner]:
+                    tell(ROUND_3, to, tp)
+                tell(ALL_OWNERS, me - 1, tp)
+                pl.semaphore_wait(relay.at[BLOCKS_1], 2)
+                tell_blocks(BLOCKS_2, 2)
+
         squares_sum = lax.fori_loop(starts[c], starts[c] + CHUNKS[c], mr_tile, squares_sum, unroll=True)
 
     row_sum = jnp.sum(squares_sum, axis=1, keepdims=True)
     line = jnp.sum(jnp.where(diagonal, row_sum, 0.0), axis=0, keepdims=True)
     squares[tp] = jnp.broadcast_to(line, (8, TOK))
+    pl.semaphore_wait(relay.at[TWO_TP], 1)
     tp_copies = []
     for d in (2, 1, 3):
         copy = pltpu.make_async_remote_copy(
@@ -302,6 +313,10 @@
         @pl.when(jnp.logical_not(last))
         def _():
             copy.wait_send()
+
+    @pl.when(jnp.logical_not(is_owner))
+    def _():
+        pl.semaphore_wait(relay.at[ALL_OWNERS], 1)
 
     own_copies = []
     for s, (dz, dx) in enumerate(OWNER_STEPS):
@@ -357,7 +372,10 @@
 
     lax.fori_loop(0, tiles, lr_tables, 0, unroll=4)
 
-    hear(2)
+    @pl.when(is_owner)
+    def _():
+        pl.semaphore_wait(relay.at[ROUND_3], 3)
+        pl.semaphore_wait(relay.at[BLOCKS_2], 2)
 
     my_owner = z_at * 4 + x_at
 
@@ -547,7 +565,7 @@
         pltpu.SemaphoreType.DMA((blocks,)),
         pltpu.SemaphoreType.DMA((2 * OWNERS,)),
         pltpu.SemaphoreType.DMA((OWNERS,)),
-        pltpu.SemaphoreType.REGULAR((2,)),
+        pltpu.SemaphoreType.REGULAR((7,)),
     ]
     in_place = pl.BlockSpec(memory_space=pl.ANY)
     out = jax.ShapeDtypeStruct((tok, channels), BF16)

time: 44.6 us -> 44.3 us (level)
    pallas_call x1, Pallas kernels: 41.7 us -> 41.3 us  [per_device(): pl.pallas_call(functools.partial(kernel, blocks, tp_size), out_shape=(out...]
where the time goes in v4:
time: 44.3 us; the launch traced here: 44.1 us
  Pallas kernels  43.4 us (98%)
  between operations  0.64 us (1%)
    pallas_call x1, Pallas kernels, per_device(): pl.pallas_call(functools.partial(kernel, blocks, tp_size), out_shape=(out...  41.3 us
    pallas_call x1, Pallas kernels, per_device(): pl.pallas_call(hand_over, out_shape=(out, out), in_specs=[in_place] * 2,...  2.16 us

profile of v4, /device:TPU:1, one launch (start us, length us, event | category | flops | bytes accessed | tf_op | source)
XLA Modules:
  0.0 44.1 jit_solution(5365923801195739999)
XLA Ops:
  0.6 41.3 %mixers.1 = (bf16[128,2048]{1,0:T(8,128)(2,1)}, bf16[128,2048]{1,0:T(8,128)(2,1)}) custom-call(bf16[128,2048]{1,0:T(8,128)(2,1)} %resid_h.1, bf16[128,2048]{1,0:T(8,128)(2,1)} %q_mr_h.1, bf16[128,2048]{1,0:T(8,128)(2,1)} %k_mr_h.1, bf16[128,2048]{1,0:T(8,128)(2,1)} %v_mr_h.1, bf16[128,128]{1,0:T(8,128)(2,1)} %taps_h.1, bf16[16,128]{1,0:T(8,128)(2,1)} %bitcast.1, ...), custom_call_target="tpu_custom_call" | custom-call | tf_op jit(solution)/shard_map/mixers/pallas_call | solution.py:572
  41.9 2.2 %hand_over.1 = (bf16[128,2048]{1,0:T(8,128)(2,1)}, bf16[128,2048]{1,0:T(8,128)(2,1)}) custom-call(bf16[128,2048]{1,0:T(8,128)(2,1)} %get-tuple-element.4.mixed, bf16[128,2048]{1,0:T(8,128)(2,1)} %get-tuple-element.5.lr_out), custom_call_target="tpu_custom_call" | custom-call | tf_op jit(solution)/shard_map/hand_over/pallas_call | solution.py:583

commit v5 on v4

--- a/solution.py
+++ b/solution.py
@@ -18,14 +18,15 @@
 POLES = 16
 BLOCK = 16
 OWNERS = 8
-CHUNKS = (4, 4, 4, 2, 2)
-
-TWO_TP, ROUND_1, ROUND_2, ROUND_3, ALL_OWNERS, BLOCKS_1, BLOCKS_2 = range(7)
-
-HAND_PIECES = 8
+CHUNKS = (4, 4, 4, 3, 1)
+
+TWO_TP, ROUND_1, ROUND_2, ROUND_3, ALL_OWNERS, BLOCKS_1, BLOCKS_2, BLOCKS_4 = range(8)
+
+HAND_PIECES = 4
 
 OWNER_STEPS = ((1, 2), (0, 2), (1, 1), (1, 3), (0, 1), (0, 3), (1, 0), (0, 0))
-BLOCK_STEPS = (4, 3, 5, 2, 6, 1, 7)
+NEAR_BLOCKS = (4, 3, 2, 1)
+FAR_BLOCKS = (5, 6, 7)
 
 
 def shared_steps(rate, residue):
@@ -84,13 +85,18 @@
     plane = me // 8
     planes = shards // 8
     beside = [plane * 8 + ((x_at + d) % 4) * 2 + core for d in (1, 3)]
-    above = [((plane + d) % planes) * 8 + x_at * 2 + core for d in (1, planes - 1)]
+    above = ((plane + 1 < planes, me + 8), (plane > 0, me - 8))
+    n_above = jnp.where(plane + 1 < planes, 1, 0) + jnp.where(plane > 0, 1, 0)
     partner = base + (1 - z_at) * 8 + x_at * 2 + core
 
     @pl.when(is_owner)
     def _():
-        for to in beside + above:
+        for to in beside:
             greet(to, tp)
+        for exists, to in above:
+            @pl.when(exists)
+            def _():
+                greet(to, tp)
 
     kv_copies = []
     for c in range(len(CHUNKS)):
@@ -109,7 +115,7 @@
         window[TOK:, cols] = (k_mr[:, cols].astype(F32) * v_mr[:, cols].astype(F32)).astype(BF16)
         if c == 0:
             ends = jnp.where(first, 0, 1) + jnp.where(last, 0, 1)
-            near = jnp.where(is_owner, 2 + 4, 2)
+            near = jnp.where(is_owner, 2 + 2 + n_above, 2)
             pl.semaphore_wait(barrier, ends + near)
 
         copy = pltpu.make_async_remote_copy(
@@ -135,16 +141,29 @@
             relay.at[word], inc=1, device_id=(to, to_tp), device_id_type=MESH
         )
 
+    def blocks_at(step):
+        return ((block + step < blocks, step), (block >= step, -step))
+
     def tell_blocks(word, step):
-        for d in (step, blocks - step):
-            tell(word, ((block + d) % blocks) * BLOCK + member, tp)
+        for exists, d in blocks_at(step):
+            @pl.when(exists)
+            def _():
+                tell(word, me + d * BLOCK, tp)
+
+    def hear_blocks(word, step):
+        up, down = blocks_at(step)
+        pl.semaphore_wait(relay.at[word], jnp.where(up[0], 1, 0) + jnp.where(down[0], 1, 0))
 
     tell(TWO_TP, me, (tp + 1) % tp_size)
 
     @pl.when(is_owner)
     def _():
-        for to in beside + above:
+        for to in beside:
             tell(ROUND_1, to, tp)
+        for exists, to in above:
+            @pl.when(exists)
+            def _():
+                tell(ROUND_1, to, tp)
 
     in_copies = {}
     for i, (name, src, dst) in enumerate((
@@ -231,12 +250,6 @@
             out = jnp.where(mask == i, stacked[i * rows : (i + 1) * rows], out)
         return out
 
-    @pl.when(is_owner)
-    def _():
-        pl.semaphore_wait(relay.at[ROUND_1], 4)
-        for to in beside + [partner]:
-            tell(ROUND_2, to, tp)
-        tell_blocks(BLOCKS_1, 1)
 
     squares_sum = jnp.zeros((TOK, LANES), F32)
     for name in ("resid", "q_mr"):
@@ -256,15 +269,21 @@
             result = result.astype(F32)
             return acc + result * result
 
-        if c == 2:
+        if c == 1:
+            @pl.when(is_owner)
+            def _():
+                pl.semaphore_wait(relay.at[ROUND_1], 2 + n_above)
+                for to in beside + [partner]:
+                    tell(ROUND_2, to, tp)
+                tell_blocks(BLOCKS_1, 1)
+
+        if c == 3:
             @pl.when(is_owner)
             def _():
                 pl.semaphore_wait(relay.at[ROUND_2], 3)
                 for to in beside + [partner]:
                     tell(ROUND_3, to, tp)
                 tell(ALL_OWNERS, me - 1, tp)
-                pl.semaphore_wait(relay.at[BLOCKS_1], 2)
-                tell_blocks(BLOCKS_2, 2)
 
         squares_sum = lax.fori_loop(starts[c], starts[c] + CHUNKS[c], mr_tile, squares_sum, unroll=True)
 
@@ -299,6 +318,12 @@
 
     lax.fori_loop(0, tiles, leave_table, 0, unroll=4)
     lax.fori_loop(0, tiles, gate_tile, 0, unroll=4)
+
+    @pl.when(is_owner)
+    def _():
+        hear_blocks(BLOCKS_1, 1)
+        tell_blocks(BLOCKS_2, 2)
+
     for copy in tp_copies:
         copy.wait_recv()
     line = squares[0, :1, :]
@@ -360,6 +385,14 @@
         else:
             copy.start()
 
+    far = 4
+    passes_far = is_owner & (block >= far) & (block < blocks - 1)
+
+    @pl.when(passes_far)
+    def _():
+        hear_blocks(BLOCKS_2, 2)
+        tell(BLOCKS_4, me - far * BLOCK, tp)
+
     def lr_conv_tile(j, carry):
         cols = pl.ds(pl.multiple_of(j * LANES, LANES), LANES)
         rows = pl.ds(pl.multiple_of(j * PER_TILE * TOK, TOK), PER_TILE * TOK)
@@ -375,7 +408,6 @@
     @pl.when(is_owner)
     def _():
         pl.semaphore_wait(relay.at[ROUND_3], 3)
-        pl.semaphore_wait(relay.at[BLOCKS_2], 2)
 
     my_owner = z_at * 4 + x_at
 
@@ -410,13 +442,28 @@
         for i in range(BLOCK):
             state = state * through + gathered[i].astype(F32)
         total[...] = state.astype(BF16)
-        for d in BLOCK_STEPS:
+
+        @pl.when(block < far)
+        def _():
+            hear_blocks(BLOCKS_2, 2)
+
+        for d in NEAR_BLOCKS:
             @pl.when(block + d < blocks)
             def _():
                 total_copy(d, block + d).start()
 
-        lax.fori_loop(0, tiles, lr_conv_tile, 0, unroll=4)
-        lax.fori_loop(0, tiles, entry_table, 0, unroll=4)
+        lax.fori_loop(0, tiles // 2, lr_conv_tile, 0, unroll=4)
+
+        @pl.when(block + far + 1 < blocks)
+        def _():
+            pl.semaphore_wait(relay.at[BLOCKS_4], 1)
+
+        for d in FAR_BLOCKS:
+            @pl.when(block + d < blocks)
+            def _():
+                total_copy(d, block + d).start()
+
+        lax.fori_loop(tiles // 2, tiles, lr_conv_tile, 0, unroll=4)
 
         carried = jnp.zeros((2 * POLES, LANES), F32)
         for b in range(blocks - 1):
@@ -441,6 +488,7 @@
                 device_id_type=MESH,
             ).start()
         carry_in[my_owner] = carry_out[member]
+        lax.fori_loop(0, tiles, entry_table, 0, unroll=4)
 
     @pl.when(jnp.logical_not(is_owner))
     def _():
@@ -490,7 +538,11 @@
 
     @pl.when(is_owner)
     def _():
-        for d in BLOCK_STEPS:
+        @pl.when(block == blocks - 1)
+        def _():
+            hear_blocks(BLOCKS_2, 2)
+
+        for d in NEAR_BLOCKS + FAR_BLOCKS:
             @pl.when(block + d < blocks)
             def _():
                 total_copy(d, block + d).wait_send()
@@ -565,7 +617,7 @@
         pltpu.SemaphoreType.DMA((blocks,)),
         pltpu.SemaphoreType.DMA((2 * OWNERS,)),
         pltpu.SemaphoreType.DMA((OWNERS,)),
-        pltpu.SemaphoreType.REGULAR((7,)),
+        pltpu.SemaphoreType.REGULAR((8,)),
     ]
     in_place = pl.BlockSpec(memory_space=pl.ANY)
     out = jax.ShapeDtypeStruct((tok, channels), BF16)

time: 44.3 us -> 40.4 us (0.912)
  Pallas kernels: 43.4 us -> 39.6 us
    pallas_call x1, Pallas kernels: 41.3 us -> 37.5 us  [per_device(): pl.pallas_call(functools.partial(kernel, blocks, tp_size), out_shape=(out...]
where the time goes in v5:
time: 40.4 us; the launch traced here: 40.2 us
  Pallas kernels  39.6 us (98%)
  between operations  0.64 us (2%)
    pallas_call x1, Pallas kernels, per_device(): pl.pallas_call(functools.partial(kernel, blocks, tp_size), out_shape=(out...  37.5 us
    pallas_call x1, Pallas kernels, per_device(): pl.pallas_call(hand_over, out_shape=(out, out), in_specs=[in_place] * 2,...  2.09 us

profile of v5, /device:TPU:1, one launch (start us, length us, event | category | flops | bytes accessed | tf_op | source)
XLA Modules:
  0.0 40.2 jit_solution(6442761066699826750)
XLA Ops:
  0.6 37.5 %mixers.1 = (bf16[128,2048]{1,0:T(8,128)(2,1)}, bf16[128,2048]{1,0:T(8,128)(2,1)}) custom-call(bf16[128,2048]{1,0:T(8,128)(2,1)} %resid_h.1, bf16[128,2048]{1,0:T(8,128)(2,1)} %q_mr_h.1, bf16[128,2048]{1,0:T(8,128)(2,1)} %k_mr_h.1, bf16[128,2048]{1,0:T(8,128)(2,1)} %v_mr_h.1, bf16[128,128]{1,0:T(8,128)(2,1)} %taps_h.1, bf16[16,128]{1,0:T(8,128)(2,1)} %bitcast.1, ...), custom_call_target="tpu_custom_call" | custom-call | tf_op jit(solution)/shard_map/mixers/pallas_call | solution.py:624
  38.2 2.1 %hand_over.1 = (bf16[128,2048]{1,0:T(8,128)(2,1)}, bf16[128,2048]{1,0:T(8,128)(2,1)}) custom-call(bf16[128,2048]{1,0:T(8,128)(2,1)} %get-tuple-element.4.mixed, bf16[128,2048]{1,0:T(8,128)(2,1)} %get-tuple-element.5.lr_out), custom_call_target="tpu_custom_call" | custom-call | tf_op jit(solution)/shard_map/hand_over/pallas_call | solution.py:635

commit v6 on v5

--- a/solution.py
+++ b/solution.py
@@ -454,15 +454,14 @@
 
         lax.fori_loop(0, tiles // 2, lr_conv_tile, 0, unroll=4)
 
-        @pl.when(block + far + 1 < blocks)
-        def _():
+        def totals_to_far():
             pl.semaphore_wait(relay.at[BLOCKS_4], 1)
-
-        for d in FAR_BLOCKS:
-            @pl.when(block + d < blocks)
-            def _():
-                total_copy(d, block + d).start()
-
+            for d in FAR_BLOCKS:
+                @pl.when(block + d < blocks)
+                def _():
+                    total_copy(d, block + d).start()
+
+        pl.when((block + far + 1 < blocks) & (block >= 2))(totals_to_far)
         lax.fori_loop(tiles // 2, tiles, lr_conv_tile, 0, unroll=4)
 
         carried = jnp.zeros((2 * POLES, LANES), F32)
@@ -489,6 +488,7 @@
             ).start()
         carry_in[my_owner] = carry_out[member]
         lax.fori_loop(0, tiles, entry_table, 0, unroll=4)
+        pl.when(block < 2)(totals_to_far)
 
     @pl.when(jnp.logical_not(is_owner))
     def _():

time: 40.4 us -> 36.8 us (0.911)
  the two profiles are of different devices: /device:TPU:1 before, /device:TPU:449 now
where the time goes in v6:
time: 36.8 us; the launch traced here: 36.6 us
  Pallas kernels  36 us (98%)
  between operations  0.64 us (2%)
    pallas_call x1, Pallas kernels, per_device(): pl.pallas_call(functools.partial(kernel, blocks, tp_size), out_shape=(out...  33.9 us
    pallas_call x1, Pallas kernels, per_device(): pl.pallas_call(hand_over, out_shape=(out, out), in_specs=[in_place] * 2,...  2.09 us

profile of v6, /device:TPU:449, one launch (start us, length us, event | category | flops | bytes accessed | tf_op | source)
XLA Modules:
  0.0 36.6 jit_solution(12274046608175769655)
XLA Ops:
  0.6 33.9 %mixers.1 = (bf16[128,2048]{1,0:T(8,128)(2,1)}, bf16[128,2048]{1,0:T(8,128)(2,1)}) custom-call(bf16[128,2048]{1,0:T(8,128)(2,1)} %resid_h.1, bf16[128,2048]{1,0:T(8,128)(2,1)} %q_mr_h.1, bf16[128,2048]{1,0:T(8,128)(2,1)} %k_mr_h.1, bf16[128,2048]{1,0:T(8,128)(2,1)} %v_mr_h.1, bf16[128,128]{1,0:T(8,128)(2,1)} %taps_h.1, bf16[16,128]{1,0:T(8,128)(2,1)} %bitcast.1, ...), custom_call_target="tpu_custom_call" | custom-call | tf_op jit(solution)/shard_map/mixers/pallas_call | solution.py:624
  34.5 2.1 %hand_over.1 = (bf16[128,2048]{1,0:T(8,128)(2,1)}, bf16[128,2048]{1,0:T(8,128)(2,1)}) custom-call(bf16[128,2048]{1,0:T(8,128)(2,1)} %get-tuple-element.4.mixed, bf16[128,2048]{1,0:T(8,128)(2,1)} %get-tuple-element.5.lr_out), custom_call_target="tpu_custom_call" | custom-call | tf_op jit(solution)/shard_map/hand_over/pallas_call | solution.py:635

commit v7 on v6

--- a/solution.py
+++ b/solution.py
@@ -303,6 +303,11 @@
         )
         copy.start()
         tp_copies.append(copy)
+    @pl.when(is_owner)
+    def _():
+        hear_blocks(BLOCKS_1, 1)
+        tell_blocks(BLOCKS_2, 2)
+
     mixed_copy = pltpu.make_async_copy(mixed, mixed_h, out_sem.at[0])
     mixed_copy.start()
     for name in ("k_lr", "gain", "q_lr"):
@@ -318,11 +323,6 @@
 
     lax.fori_loop(0, tiles, leave_table, 0, unroll=4)
     lax.fori_loop(0, tiles, gate_tile, 0, unroll=4)
-
-    @pl.when(is_owner)
-    def _():
-        hear_blocks(BLOCKS_1, 1)
-        tell_blocks(BLOCKS_2, 2)
 
     for copy in tp_copies:
         copy.wait_recv()
@@ -452,7 +452,7 @@
             def _():
                 total_copy(d, block + d).start()
 
-        lax.fori_loop(0, tiles // 2, lr_conv_tile, 0, unroll=4)
+        lax.fori_loop(0, tiles // 4, lr_conv_tile, 0, unroll=4)
 
         def totals_to_far():
             pl.semaphore_wait(relay.at[BLOCKS_4], 1)
@@ -462,7 +462,7 @@
                     total_copy(d, block + d).start()
 
         pl.when((block + far + 1 < blocks) & (block >= 2))(totals_to_far)
-        lax.fori_loop(tiles // 2, tiles, lr_conv_tile, 0, unroll=4)
+        lax.fori_loop(tiles // 4, tiles, lr_conv_tile, 0, unroll=4)
 
         carried = jnp.zeros((2 * POLES, LANES), F32)
         for b in range(blocks - 1):
@@ -487,8 +487,9 @@
                 device_id_type=MESH,
             ).start()
         carry_in[my_owner] = carry_out[member]
+        pl.when(block == 1)(totals_to_far)
         lax.fori_loop(0, tiles, entry_table, 0, unroll=4)
-        pl.when(block < 2)(totals_to_far)
+        pl.when(block == 0)(totals_to_far)
 
     @pl.when(jnp.logical_not(is_owner))
     def _():

time: 36.8 us -> 36.8 us (level)
  no operation moved by 1% of the time
where the time goes in v7:
time: 36.8 us; the launch traced here: 36.6 us
  Pallas kernels  36 us (98%)
  between operations  0.64 us (2%)
    pallas_call x1, Pallas kernels, per_device(): pl.pallas_call(functools.partial(kernel, blocks, tp_size), out_shape=(out...  33.9 us
    pallas_call x1, Pallas kernels, per_device(): pl.pallas_call(hand_over, out_shape=(out, out), in_specs=[in_place] * 2,...  2.09 us

profile of v7, /device:TPU:449, one launch (start us, length us, event | category | flops | bytes accessed | tf_op | source)
XLA Modules:
  0.0 36.6 jit_solution(6431468533245802692)
XLA Ops:
  0.6 33.9 %mixers.1 = (bf16[128,2048]{1,0:T(8,128)(2,1)}, bf16[128,2048]{1,0:T(8,128)(2,1)}) custom-call(bf16[128,2048]{1,0:T(8,128)(2,1)} %resid_h.1, bf16[128,2048]{1,0:T(8,128)(2,1)} %q_mr_h.1, bf16[128,2048]{1,0:T(8,128)(2,1)} %k_mr_h.1, bf16[128,2048]{1,0:T(8,128)(2,1)} %v_mr_h.1, bf16[128,128]{1,0:T(8,128)(2,1)} %taps_h.1, bf16[16,128]{1,0:T(8,128)(2,1)} %bitcast.1, ...), custom_call_target="tpu_custom_call" | custom-call | tf_op jit(solution)/shard_map/mixers/pallas_call | solution.py:625
  34.5 2.1 %hand_over.1 = (bf16[128,2048]{1,0:T(8,128)(2,1)}, bf16[128,2048]{1,0:T(8,128)(2,1)}) custom-call(bf16[128,2048]{1,0:T(8,128)(2,1)} %get-tuple-element.4.mixed, bf16[128,2048]{1,0:T(8,128)(2,1)} %get-tuple-element.5.lr_out), custom_call_target="tpu_custom_call" | custom-call | tf_op jit(solution)/shard_map/hand_over/pallas_call | solution.py:636
